TPU v7x, 32 devices: a whole 2x2x4 slice. The times are simulated.
32 devices in a mesh: ctx: 8 (over z, x), kvh: 4 (over y, core).
Axes of the slice: x: 2, y: 2, z: 4, core: 2. Of those that a mesh axis runs over, the one named last changes fastest.
Arguments:
- queries: bfloat16 [2048, 64, 128], P('ctx', 'kvh'), may hold values from -6 to 6
- keys: bfloat16 [2048, 8, 128], P(('ctx', 'kvh')), may hold values from -6 to 6
- values: bfloat16 [2048, 8, 128], P(('ctx', 'kvh')), may hold values from -6 to 6
- doc_blocks: int32 [4], replicated, may hold values from 1 to 6, 16 in all
Outputs:
- attended: bfloat16 [2048, 64, 128], P('ctx', 'kvh')
Inputs may be any that keep to these rules, and one draw needn't show every extreme that they name: document i covers doc_blocks[i] * 128 tokens; the lengths sum to 2048 tokens.
All inputs are finite; a program needn't handle non-finite values.
Results may differ from a plain program's by a relative error of at most 0.004.
Values may be sent and summed in bfloat16 or wider, within the bound.
No kernel may reach another device: no remote copies, remote signals or barrier semaphores. Data moves between devices by JAX's collectives and lax.ppermute only.
A program may use at most 64 MiB of HBM per device.

v0:
```python
import functools
import math

import jax
import jax.numpy as jnp
from jax import lax
from jax.experimental import pallas as pl
from jax.experimental.pallas import tpu as pltpu
from jax.sharding import PartitionSpec as P

BLOCK = 128
CHUNK = 16
TOGETHER = 8
lowest = -1e30


def passed_along(shard, axis, by):
    size = lax.axis_size(axis)
    pairs = [(i, i + by) for i in range(size) if 0 <= i + by < size]
    return lax.ppermute(shard, axis, pairs)


def plan_kernel(docs_ref, index_ref, spans_ref, behind_ref):
    blocks = behind_ref.shape[0]
    first = index_ref[0] * blocks
    spans, start = jnp.int32(0), jnp.int32(0)
    behind = [jnp.int32(0)] * blocks
    for i in range(docs_ref.shape[0]):
        for block in range(blocks):
            behind[block] = jnp.where(first + block >= start, first + block - start, behind[block])
        end = start + docs_ref[i]
        spans = jnp.maximum(spans, lax.div(end - 1, blocks) - lax.div(start, blocks))
        start = end
    spans_ref[0] = spans
    for block in range(blocks):
        behind_ref[block] = jnp.full(behind_ref.shape[1:], behind[block], jnp.int32)


def fill(shard_refs, key_win, value_win):
    at = 0
    for ref in reversed(shard_refs):
        pieces, count, tokens, depth = ref.shape
        depth = depth // 2
        group = BLOCK // tokens
        for piece in range(0, pieces, group):
            for head in range(count):
                lanes = slice(head * depth, (head + 1) * depth)
                key, value = (
                    jnp.concatenate([ref[piece + i, head, :, half] for i in range(group)], axis=0)
                    for half in (slice(0, depth), slice(depth, 2 * depth))
                )
                key_win[lanes, at : at + BLOCK] = key.T
                value_win[at : at + BLOCK, lanes] = value
            at += BLOCK


def key_scores(count, heads, query, keys):
    head_of = lax.broadcasted_iota(jnp.int32, query.shape, 0) % heads // (heads // count)
    spread = jnp.concatenate(
        [jnp.where(head_of == head, query, jnp.zeros_like(query)) for head in range(count)], axis=1
    )
    return jnp.dot(spread, keys, preferred_element_type=jnp.float32)


def value_sums(count, heads, weights, values):
    wide = jnp.dot(weights.astype(jnp.bfloat16), values, preferred_element_type=jnp.float32)
    depth = wide.shape[1] // count
    tall = wide.reshape(wide.shape[0] // heads, count, heads // count, wide.shape[1])
    return jnp.concatenate(
        [tall[:, head : head + 1, :, head * depth : (head + 1) * depth] for head in range(count)], axis=1
    ).reshape(wide.shape[0], depth)


def lane_sums(weights):
    return sum(weights[:, at : at + BLOCK] for at in range(0, weights.shape[1], BLOCK))


def in_chunks(blocks, work):
    steps = BLOCK // CHUNK

    def together(some, carry):
        for step in range(TOGETHER):
            for block in range(blocks):
                work(block, some * TOGETHER + step)
        return carry

    if TOGETHER == steps:
        together(0, None)
    else:
        lax.fori_loop(0, steps // TOGETHER, together, None)


def own_kernel(scale, behind_ref, query_ref, shard_ref, summed_ref, top_ref, total_ref, key_win, value_win):
    rows, heads, depth = query_ref.shape
    count = shard_ref.shape[1]
    blocks = rows // BLOCK
    behind = [jnp.max(behind_ref[block]) for block in range(blocks)]
    fill([shard_ref], key_win, value_win)
    chunk_rows = CHUNK * heads
    ahead = lax.broadcasted_iota(jnp.int32, (chunk_rows, BLOCK), 1)
    ahead = ahead - lax.broadcasted_iota(jnp.int32, (chunk_rows, BLOCK), 0) // heads

    def work(numbers, block, step):
        start, width = (block - numbers[block]) * BLOCK, (numbers[block] + 1) * BLOCK
        first = block * BLOCK + step * CHUNK
        query = query_ref[pl.ds(first, CHUNK)].reshape(chunk_rows, depth)
        scores = key_scores(count, heads, query, key_win[:, start : start + width])
        last = jnp.where(ahead <= step * CHUNK, scores[:, width - BLOCK :], lowest)
        scores = jnp.concatenate([scores[:, : width - BLOCK], last], axis=1) if width > BLOCK else last
        top = jnp.max(scores, axis=1, keepdims=True)
        weights = jnp.exp2((scores - top) * (scale * math.log2(math.e)))
        at = pl.ds(pl.multiple_of(first * heads, chunk_rows), chunk_rows)
        top_ref[at] = jnp.broadcast_to(top, (chunk_rows, BLOCK))
        total_ref[at] = lane_sums(weights)
        summed_ref[at] = value_sums(count, heads, weights, value_win[start : start + width])

    joint = behind[1] >= 1 if blocks == 2 else None
    for same in (True, False):

        @pl.when(joint if same else jnp.logical_not(joint))
        def _():
            numbers = (0, int(same))
            in_chunks(blocks, functools.partial(work, numbers))


def join_kernel(scale, offset, final, behind_ref, query_ref, summed_in, top_in, total_in, *refs):
    outs = 1 if final else 3
    if final:
        *shard_refs, out_to, key_win, value_win, out_ref, left = refs
    else:
        shard_refs, (*out_refs, key_win, value_win) = refs[: -outs - 2], refs[-outs - 2 :]
    rows, heads, depth = query_ref.shape
    count = shard_refs[0].shape[1]
    blocks = rows // BLOCK
    window = value_win.shape[0] // BLOCK
    behind = [jnp.max(behind_ref[block]) for block in range(blocks)]
    fars = [jnp.clip(behind[block] - offset - block, 0, window) for block in range(blocks)]
    fill(shard_refs, key_win, value_win)
    chunk_rows = CHUNK * heads
    rate = scale * math.log2(math.e)

    def work(taking, block, step):
        first = block * BLOCK + step * CHUNK
        at = pl.ds(pl.multiple_of(first * heads, chunk_rows), chunk_rows)
        if taking[block]:
            start = (window - taking[block]) * BLOCK
            query = query_ref[pl.ds(first, CHUNK)].reshape(chunk_rows, depth)
            scores = key_scores(count, heads, query, key_win[:, start:]) + hidden[block][:, start:]
            top_old = top_in[at]
            top = jnp.maximum(top_old, jnp.max(scores, axis=1, keepdims=True))
            fading = jnp.exp2((top_old - top) * rate)
            weights = jnp.exp2((scores - jnp.concatenate([top] * taking[block], axis=1)) * rate)
            total = total_in[at] * fading + lane_sums(weights)
            summed = summed_in[at] * fading + value_sums(count, heads, weights, value_win[start:])
        elif final:
            summed, total = summed_in[at], total_in[at]
        else:
            summed, top, total = summed_in[at], top_in[at], total_in[at]
        if final:
            out = (summed / jnp.sum(total, axis=1, keepdims=True)).astype(out_ref.dtype)
            out_ref[pl.ds(first, CHUNK)] = out.reshape(CHUNK, heads, depth)
            at = pl.ds(first, CHUNK)
            pltpu.make_async_copy(out_ref.at[at], out_to.at[at], left).start()
        else:
            for ref, value in zip(out_refs, (summed, top, total)):
                ref[at] = value

    column = lax.broadcasted_iota(jnp.int32, (1, window * BLOCK), 1)
    hidden = [jnp.where(column < (window - far) * BLOCK, lowest, 0.0) for far in fars]
    levels = sorted({0, min(2, window), window})
    even = window - window % 2
    cases = [(0, 0)] + [(n, m) for n in levels[1:] for m in sorted({0, 2, min(n, even)})]
    needed = [sum(jnp.where(far > low, high - low, 0) for low, high in zip(levels, levels[1:])) for far in fars]
    needed[1] = jnp.minimum(needed[1], even)
    for taking in cases:

        @pl.when(jnp.logical_and(needed[0] == taking[0], needed[1] == taking[1]))
        def _():
            in_chunks(blocks, functools.partial(work, taking))

    if final:
        pltpu.make_async_copy(out_ref, out_to, left).wait()


def body(queries, keys, values, doc_blocks):
    tokens, kv_heads, depth = keys.shape
    parts = lax.axis_size("kvh")
    count = kv_heads // parts
    rows, heads, _ = queries.shape
    sections = min(3, lax.axis_size("ctx") // 4)
    behind = 2**sections - 1
    per_shard = rows // BLOCK
    smem, vmem = pl.BlockSpec(memory_space=pltpu.SMEM), pl.BlockSpec(memory_space=pltpu.VMEM)
    params = pltpu.CompilerParams(vmem_limit_bytes=24 * 1024 * 1024)
    scale = 1.0 / math.sqrt(depth)
    light, heavy = (
        pl.CostEstimate(flops=flops, bytes_accessed=2**20, transcendentals=10**6) for flops in (10**8, 4 * 10**10)
    )
    shape = jax.ShapeDtypeStruct
    index = lax.axis_index("ctx").astype(jnp.int32).reshape(1)
    spans, nearer = pl.pallas_call(
        plan_kernel,
        out_shape=(shape((1,), jnp.int32), shape((per_shard, 8, 128), jnp.int32)),
        in_specs=[smem] * 2,
        out_specs=(smem, vmem),
        cost_estimate=light,
        name="plan",
    )(doc_blocks, index)
    both = lax.optimization_barrier(jnp.concatenate([keys, values], axis=2))
    both = both.reshape(tokens, parts, count, 2 * depth).transpose(1, 2, 0, 3)
    own = lax.all_to_all(both, "kvh", split_axis=0, concat_axis=0, tiled=True)
    far = [passed_along(own, "ctx", 2)]
    one = passed_along(own, "ctx", 1)
    for distance in range(3, behind + 1):
        sent = own if distance < behind else own[parts // 2 :]
        send = functools.partial(passed_along, axis="ctx", by=distance)
        far.append(lax.cond(spans[0] >= distance, send, lambda x: x, sent))
    own, far[1:] = lax.optimization_barrier((own, far[1:]))

    state = [shape((rows * heads, depth), jnp.float32)] * 3

    def window(group):
        length = sum(s.shape[0] * s.shape[2] for s in group)
        return [
            pltpu.VMEM((count * depth, length), jnp.bfloat16),
            pltpu.VMEM((length, count * depth), jnp.bfloat16),
        ]

    kept = pl.pallas_call(
        functools.partial(own_kernel, scale),
        out_shape=state,
        in_specs=[vmem] * 3,
        out_specs=[vmem] * 3,
        scratch_shapes=window([own]),
        compiler_params=params,
        cost_estimate=light,
        name="own",
    )(nearer, queries, own)
    kept = pl.pallas_call(
        functools.partial(join_kernel, scale, 0, False),
        out_shape=state,
        in_specs=[vmem] * 6,
        out_specs=[vmem] * 3,
        scratch_shapes=window([one]),
        compiler_params=params,
        cost_estimate=heavy,
        name="one",
    )(nearer, queries, *kept, one)
    return pl.pallas_call(
        functools.partial(join_kernel, scale, per_shard, True),
        out_shape=shape(queries.shape, queries.dtype),
        in_specs=[vmem] * (5 + len(far)),
        out_specs=pl.BlockSpec(memory_space=pl.ANY),
        scratch_shapes=window(far) + [pltpu.VMEM(queries.shape, queries.dtype), pltpu.SemaphoreType.DMA],
        compiler_params=params,
        cost_estimate=light,
        name="far",
    )(nearer, queries, *kept, *far)


def solution(mesh):
    in_specs = (
        P("ctx", "kvh", None),
        P(("ctx", "kvh"), None, None),
        P(("ctx", "kvh"), None, None),
        P(),
    )
    out_specs = P("ctx", "kvh", None)
    return jax.shard_map(body, mesh=mesh, in_specs=in_specs, out_specs=out_specs, check_vma=False)
```

profile of v0, /device:TPU:10, one launch (start us, length us, event | category | flops | bytes accessed | tf_op | source)
XLA Modules:
  0.0 28.5 jit_solution(17622534811836474810)
XLA Ops:
  0.0 0.0 copy-start
  0.0 1.1 %pad_maximum_fusion = bf16[64,8,256]{2,1,0:T(8,128)(2,1)S(1)} fusion(bf16[64,8,128]{2,1,0:T(8,128)(2,1)} %param.8, bf16[64,8,128]{2,1,0:T(8,128)(2,1)} %param.7), kind=kLoop, calls=%fused_computation | loop fusion | flops 524288 | bytes 524288 | tf_op jit(solution)/shard_map/concatenate | solution.py:209
  1.1 8.6 %all_to_all.5.shard_ref = bf16[4,2,64,256]{3,2,1,0:T(8,128)(2,1)S(1)} all-to-all(bf16[4,2,64,256]{3,2,1,0:T(8,128)(2,1)S(1)} %bitcast.5), channel_id=1, replica_groups=mesh['ctx'=8,'kvh'=4] {'kvh'}, dimensions={0} | all-to-all | bytes 524288 | tf_op jit(solution)/shard_map/all_to_all | solution.py:211
  9.8 3.4 %collective-permute-start.1 = (bf16[4,2,64,256]{3,2,1,0:T(8,128)(2,1)S(1)}, bf16[4,2,64,256]{3,2,1,0:T(8,128)(2,1)S(1)}, u32[]{:S(2)}, u32[]{:S(2)}) collective-permute-start(bf16[4,2,64,256]{3,2,1,0:T(8,128)(2,1)S(1)} %all_to_all.5.shard_ref), channel_id=1, source_target_pairs={{0,4},{4,8},{8,12},{12,16},{16,20},{20,24},{24,28},{1,5},{5,9},{9,... | collective-permute-start | bytes 786440 | tf_op jit(solution)/shard_map/ppermute | solution.py:20
  13.2 1.3 %plan.1 = (s32[1]{0:T(128)}, s32[2,8,128]{2,1,0:T(8,128)}) custom-call(s32[4]{0:T(128)} %docs_ref.1, s32[1]{0:T(128)} %bitcast.index_ref), custom_call_target="tpu_custom_call" | custom-call | flops 100000000 | bytes 1048576 | tf_op jit(solution)/shard_map/plan/pallas_call | solution.py:201
  15.2 3.5 %collective-permute-start.2 = (bf16[4,2,64,256]{3,2,1,0:T(8,128)(2,1)S(1)}, bf16[4,2,64,256]{3,2,1,0:T(8,128)(2,1)S(1)}, u32[]{:S(2)}, u32[]{:S(2)}) collective-permute-start(bf16[4,2,64,256]{3,2,1,0:T(8,128)(2,1)S(1)} %all_to_all.5.shard_ref), channel_id=1, source_target_pairs={{0,8},{4,12},{8,16},{12,20},{16,24},{20,28},{1,9},{5,13},{9,17},{1... | collective-permute-start | bytes 786440 | tf_op jit(solution)/shard_map/ppermute | solution.py:20
  18.7 0.0 copy-done
  18.7 0.0 copy-start.1
  18.7 0.7 %copy-done.1 = s32[2,8,128]{2,1,0:T(8,128)S(1)} copy-done((s32[2,8,128]{2,1,0:T(8,128)S(1)}, s32[2,8,128]{2,1,0:T(8,128)}, u32[]{:S(2)}) %copy-start.1) | copy-done | bytes 8216
  19.4 1.6 %own.1 = (f32[4096,128]{1,0:T(8,128)S(1)}, f32[4096,128]{1,0:T(8,128)S(1)}, f32[4096,128]{1,0:T(8,128)S(1)}) custom-call(s32[2,8,128]{2,1,0:T(8,128)S(1)} %copy-done.1, bf16[256,16,128]{2,1,0:T(8,128)(2,1)S(1)} %copy-done, bf16[4,2,64,256]{3,2,1,0:T(8,128)(2,1)S(1)} %all_to_all.5.shard_ref), custom_call_target="tpu_custom_call" | custom-call | flops 100000000 | bytes 1048576 | tf_op jit(solution)/shard_map/own/pallas_call | solution.py:229
  21.0 0.0 collective-permute-done.1.refs_0_
  21.1 2.4 %one.1 = (f32[4096,128]{1,0:T(8,128)S(1)}, f32[4096,128]{1,0:T(8,128)S(1)}, f32[4096,128]{1,0:T(8,128)S(1)}) custom-call(s32[2,8,128]{2,1,0:T(8,128)S(1)} %copy-done.1, bf16[256,16,128]{2,1,0:T(8,128)(2,1)S(1)} %copy-done, f32[4096,128]{1,0:T(8,128)S(1)} %get-tuple-element.23.summed_in, f32[4096,128]{1,0:T(8,128)S(1)} %get-tuple-element.24.top_in, ...), custom_call_target="tpu_custom_call" | custom-call | flops 40000000000 | bytes 1048576 | tf_op jit(solution)/shard_map/one/pallas_call | solution.py:239
  23.4 1.5 %collective-permute-done.2.refs_0_ = bf16[4,2,64,256]{3,2,1,0:T(8,128)(2,1)S(1)} collective-permute-done((bf16[4,2,64,256]{3,2,1,0:T(8,128)(2,1)S(1)}, bf16[4,2,64,256]{3,2,1,0:T(8,128)(2,1)S(1)}, u32[]{:S(2)}, u32[]{:S(2)}) %collective-permute-start.2) | collective-permute-done | bytes 262176 | tf_op jit(solution)/shard_map/ppermute | solution.py:20
  24.9 3.4 %far.1 = bf16[256,16,128]{2,1,0:T(8,128)(2,1)} custom-call(s32[2,8,128]{2,1,0:T(8,128)S(1)} %copy-done.1, bf16[256,16,128]{2,1,0:T(8,128)(2,1)S(1)} %copy-done, f32[4096,128]{1,0:T(8,128)S(1)} %get-tuple-element.26.summed_in, f32[4096,128]{1,0:T(8,128)S(1)} %get-tuple-element.27.top_in, f32[4096,128]{1,0:T(8,128)S(1)} %get-tuple-element.28.total_in, ...), custom_call_target="tpu_custom_call" | custom-call | flops 100000000 | bytes 1048576 | tf_op jit(solution)/shard_map/far/pallas_call | solution.py:249
  (3 shorter events, 0.1 us)
Async XLA Ops:
  0.0 18.7 %copy-start = (bf16[256,16,128]{2,1,0:T(8,128)(2,1)S(1)}, bf16[256,16,128]{2,1,0:T(8,128)(2,1)}, u32[]{:S(2)}) copy-start(bf16[256,16,128]{2,1,0:T(8,128)(2,1)} %query_ref.5) | copy-start | bytes 3145732
  9.8 11.3 %collective-permute-start.1 = (bf16[4,2,64,256]{3,2,1,0:T(8,128)(2,1)S(1)}, bf16[4,2,64,256]{3,2,1,0:T(8,128)(2,1)S(1)}, u32[]{:S(2)}, u32[]{:S(2)}) collective-permute-start(bf16[4,2,64,256]{3,2,1,0:T(8,128)(2,1)S(1)} %all_to_all.5.shard_ref), channel_id=1, source_target_pairs={{0,4},{4,8},{8,12},{12,16},{16,20},{20,24},{24,28},{1,5},{5,9},{9,... | collective-permute-start | bytes 786440 | tf_op jit(solution)/shard_map/ppermute | solution.py:20
  15.2 9.7 %collective-permute-start.2 = (bf16[4,2,64,256]{3,2,1,0:T(8,128)(2,1)S(1)}, bf16[4,2,64,256]{3,2,1,0:T(8,128)(2,1)S(1)}, u32[]{:S(2)}, u32[]{:S(2)}) collective-permute-start(bf16[4,2,64,256]{3,2,1,0:T(8,128)(2,1)S(1)} %all_to_all.5.shard_ref), channel_id=1, source_target_pairs={{0,8},{4,12},{8,16},{12,20},{16,24},{20,28},{1,9},{5,13},{9,17},{1... | collective-permute-start | bytes 786440 | tf_op jit(solution)/shard_map/ppermute | solution.py:20
  18.7 0.7 %copy-start.1 = (s32[2,8,128]{2,1,0:T(8,128)S(1)}, s32[2,8,128]{2,1,0:T(8,128)}, u32[]{:S(2)}) copy-start(s32[2,8,128]{2,1,0:T(8,128)} %get-tuple-element.20.behind_ref) | copy-start | bytes 24580
where the time goes:
time: 28.8 us; the launch traced here: 28.5 us
  Pallas kernels  8.69 us (30%)
  blocking collectives  8.63 us (30%)
  starting transfers between devices  6.93 us (24%)
  waiting for transfers between devices  1.51 us (5%)
  other arithmetic  1.09 us (4%)
  between operations  0.88 us (3%)
  local copies, waits for them, and re-layouts  0.76 us (3%)
    all_to_all x1, blocking collectives, body(): own = lax.all_to_all(both, 'kvh', split_axis=0, concat_axis=0, tiled=True)  8.63 us
    ppermute x2, starting transfers between devices, passed_along(): return lax.ppermute(shard, axis, pairs)  6.93 us
    pallas_call x1, Pallas kernels, body(): pl.pallas_call(functools.partial(join_kernel, scale, per_shard, True), ou...  3.4 us
    pallas_call x1, Pallas kernels, body(): pl.pallas_call(functools.partial(join_kernel, scale, 0, False), out_shape...  2.36 us
    pallas_call x1, Pallas kernels, body(): pl.pallas_call(functools.partial(own_kernel, scale), out_shape=state, in_...  1.64 us
    ppermute x2, waiting for transfers between devices, passed_along(): return lax.ppermute(shard, axis, pairs)  1.51 us
    pallas_call x1, Pallas kernels, body(): pl.pallas_call(plan_kernel, out_shape=(shape((1,), jnp.int32), shape((per...  1.29 us
    concatenate x1, other arithmetic, body(): both = lax.optimization_barrier(jnp.concatenate([keys, values], axis=2))  1.09 us
  transfers between devices with their start and end apart: 2, of which 1 were waited for; matrix products, arithmetic and copies ran while one was open for 0% of the time, Pallas kernels for 19%

commit v1 on v0

--- a/solution.py
+++ b/solution.py
@@ -14,29 +14,52 @@
 lowest = -1e30
 
 
-def passed_along(shard, axis, by):
+def passed_along(shard, axis, by, parity=None):
     size = lax.axis_size(axis)
-    pairs = [(i, i + by) for i in range(size) if 0 <= i + by < size]
+    pairs = [(i, (i + by) % size) for i in range(size)]
+    if parity is not None:
+        pairs = [(i, far if i % 2 == parity else i ^ 1) for i, far in pairs]
     return lax.ppermute(shard, axis, pairs)
 
 
-def plan_kernel(docs_ref, index_ref, spans_ref, behind_ref):
-    blocks = behind_ref.shape[0]
-    first = index_ref[0] * blocks
-    spans, start = jnp.int32(0), jnp.int32(0)
+def exchanged(pieces, axis):
+    size = lax.axis_size(axis)
+    me = lax.axis_index(axis)
+    bits = size.bit_length() - 1
+    shape = pieces.shape
+    pieces = pieces.reshape(*[2] * bits, *shape[1:])
+    for bit in range(bits):
+        flipped = jnp.flip(pieces, bits - 1 - bit)
+        pieces = jnp.where((me >> bit) & 1 == 1, flipped, pieces)
+    pieces = pieces.reshape(shape)
+    held = [pieces[0]]
+    for other in range(1, size):
+        held.append(lax.ppermute(pieces[other], axis, [(i, i ^ other) for i in range(size)]))
+    return jnp.stack(held)
+
+
+def plan_kernel(parts, longest, docs_ref, index_ref, spans_ref, last_ref, behind_ref):
+    blocks = behind_ref.shape[0] - 1
+    first = lax.div(index_ref[0], parts) * blocks
+    spans, even, odd, start = jnp.int32(0), jnp.int32(0), jnp.int32(0), jnp.int32(0)
     behind = [jnp.int32(0)] * blocks
     for i in range(docs_ref.shape[0]):
         for block in range(blocks):
             behind[block] = jnp.where(first + block >= start, first + block - start, behind[block])
         end = start + docs_ref[i]
-        spans = jnp.maximum(spans, lax.div(end - 1, blocks) - lax.div(start, blocks))
+        head = lax.div(start, blocks)
+        span = lax.div(end - 1, blocks) - head
+        spans = jnp.maximum(spans, span)
+        even = jnp.where((span >= longest) & (head % 2 == 0), 1, even)
+        odd = jnp.where((span >= longest) & (head % 2 == 1), 2, odd)
         start = end
     spans_ref[0] = spans
-    for block in range(blocks):
-        behind_ref[block] = jnp.full(behind_ref.shape[1:], behind[block], jnp.int32)
-
-
-def fill(shard_refs, key_win, value_win):
+    last_ref[0] = even + odd
+    for row, number in enumerate((*behind, lax.rem(index_ref[0], parts))):
+        behind_ref[row] = jnp.full(behind_ref.shape[1:], number, jnp.int32)
+
+
+def fill(me, shard_refs, key_win, value_win):
     at = 0
     for ref in reversed(shard_refs):
         pieces, count, tokens, depth = ref.shape
@@ -46,7 +69,7 @@
             for head in range(count):
                 lanes = slice(head * depth, (head + 1) * depth)
                 key, value = (
-                    jnp.concatenate([ref[piece + i, head, :, half] for i in range(group)], axis=0)
+                    jnp.concatenate([ref[((piece + i) ^ me) % pieces, head, :, half] for i in range(group)], axis=0)
                     for half in (slice(0, depth), slice(depth, 2 * depth))
                 )
                 key_win[lanes, at : at + BLOCK] = key.T
@@ -94,8 +117,8 @@
     rows, heads, depth = query_ref.shape
     count = shard_ref.shape[1]
     blocks = rows // BLOCK
-    behind = [jnp.max(behind_ref[block]) for block in range(blocks)]
-    fill([shard_ref], key_win, value_win)
+    *behind, me = [jnp.max(behind_ref[row]) for row in range(blocks + 1)]
+    fill(me, [shard_ref], key_win, value_win)
     chunk_rows = CHUNK * heads
     ahead = lax.broadcasted_iota(jnp.int32, (chunk_rows, BLOCK), 1)
     ahead = ahead - lax.broadcasted_iota(jnp.int32, (chunk_rows, BLOCK), 0) // heads
@@ -133,9 +156,9 @@
     count = shard_refs[0].shape[1]
     blocks = rows // BLOCK
     window = value_win.shape[0] // BLOCK
-    behind = [jnp.max(behind_ref[block]) for block in range(blocks)]
+    *behind, me = [jnp.max(behind_ref[row]) for row in range(blocks + 1)]
     fars = [jnp.clip(behind[block] - offset - block, 0, window) for block in range(blocks)]
-    fill(shard_refs, key_win, value_win)
+    fill(me, shard_refs, key_win, value_win)
     chunk_rows = CHUNK * heads
     rate = scale * math.log2(math.e)
 
@@ -197,24 +220,28 @@
         pl.CostEstimate(flops=flops, bytes_accessed=2**20, transcendentals=10**6) for flops in (10**8, 4 * 10**10)
     )
     shape = jax.ShapeDtypeStruct
-    index = lax.axis_index("ctx").astype(jnp.int32).reshape(1)
-    spans, nearer = pl.pallas_call(
-        plan_kernel,
-        out_shape=(shape((1,), jnp.int32), shape((per_shard, 8, 128), jnp.int32)),
+    me = lax.axis_index("kvh")
+    index = (lax.axis_index("ctx") * parts + me).astype(jnp.int32).reshape(1)
+    spans, last, nearer = pl.pallas_call(
+        functools.partial(plan_kernel, parts, behind),
+        out_shape=(shape((1,), jnp.int32), shape((1,), jnp.int32), shape((per_shard + 1, 8, 128), jnp.int32)),
         in_specs=[smem] * 2,
-        out_specs=(smem, vmem),
+        out_specs=(smem, smem, vmem),
         cost_estimate=light,
         name="plan",
     )(doc_blocks, index)
     both = lax.optimization_barrier(jnp.concatenate([keys, values], axis=2))
     both = both.reshape(tokens, parts, count, 2 * depth).transpose(1, 2, 0, 3)
-    own = lax.all_to_all(both, "kvh", split_axis=0, concat_axis=0, tiled=True)
+    own = exchanged(both, "kvh")
     far = [passed_along(own, "ctx", 2)]
     one = passed_along(own, "ctx", 1)
-    for distance in range(3, behind + 1):
-        sent = own if distance < behind else own[parts // 2 :]
+    for distance in range(3, behind):
         send = functools.partial(passed_along, axis="ctx", by=distance)
-        far.append(lax.cond(spans[0] >= distance, send, lambda x: x, sent))
+        far.append(lax.cond(spans[0] >= distance, send, lambda x: x, own))
+    half = parts // 2
+    sent = jnp.where(me >= half, own[:half], own[half:])
+    sends = [functools.partial(passed_along, axis="ctx", by=behind, parity=parity) for parity in (0, 1, None)]
+    far.append(lax.switch(last[0], [lambda x: x, *sends], sent))
     own, far[1:] = lax.optimization_barrier((own, far[1:]))
 
     state = [shape((rows * heads, depth), jnp.float32)] * 3

time: 28.8 us -> 25.2 us (0.88)
  the two profiles are of different devices: /device:TPU:10 before, /device:TPU:6 now
where the time goes in v1:
time: 25.2 us; the launch traced here: 24.8 us
  waiting for transfers between devices  9.61 us (38%)
  Pallas kernels  7.07 us (28%)
  starting transfers between devices  5.15 us (20%)
  other arithmetic  1.16 us (5%)
  between operations  0.91 us (4%)
  local copies, waits for them, and re-layouts  0.88 us (3%)
    ppermute x2, waiting for transfers between devices, passed_along(): return lax.ppermute(shard, axis, pairs)  5.68 us
    ppermute x3, waiting for transfers between devices, exchanged(): lax.ppermute(pieces[other], axis, [(i, i ^ other) for i in range(size)])  3.94 us
    ppermute x2, starting transfers between devices, passed_along(): return lax.ppermute(shard, axis, pairs)  3.23 us
    pallas_call x1, Pallas kernels, body(): pl.pallas_call(functools.partial(join_kernel, scale, 0, False), out_shape...  2.44 us
    ppermute x3, starting transfers between devices, exchanged(): lax.ppermute(pieces[other], axis, [(i, i ^ other) for i in range(size)])  1.92 us
    pallas_call x1, Pallas kernels, body(): pl.pallas_call(functools.partial(own_kernel, scale), out_shape=state, in_...  1.75 us
    pallas_call x1, Pallas kernels, body(): pl.pallas_call(functools.partial(join_kernel, scale, per_shard, True), ou...  1.58 us
    pallas_call x1, Pallas kernels, body(): pl.pallas_call(functools.partial(plan_kernel, parts, behind), out_shape=(...  1.31 us
  transfers between devices with their start and end apart: 5, of which 4 were waited for; matrix products, arithmetic and copies ran while one was open for 0% of the time, Pallas kernels for 22%

profile of v1, /device:TPU:6, one launch (start us, length us, event | category | flops | bytes accessed | tf_op | source)
XLA Modules:
  0.0 24.8 jit_solution(4909563580865842795)
XLA Ops:
  0.0 1.0 %pad_maximum_fusion = bf16[64,8,256]{2,1,0:T(8,128)(2,1)S(1)} fusion(bf16[64,8,128]{2,1,0:T(8,128)(2,1)} %param.10, bf16[64,8,128]{2,1,0:T(8,128)(2,1)} %param.9), kind=kLoop, calls=%fused_computation.2 | loop fusion | flops 524288 | bytes 524288 | tf_op jit(solution)/shard_map/concatenate | solution.py:233
  1.0 0.1 reshape.16
  1.2 0.1 reverse_select_fusion.1
  1.3 0.0 copy-start
  1.3 0.1 collective-permute-start.5
  1.4 1.5 %collective-permute-start.4 = (bf16[2,64,256]{2,1,0:T(8,128)(2,1)S(1)}, bf16[2,64,256]{2,1,0:T(8,128)(2,1)S(1)}, u32[]{:S(2)}, u32[]{:S(2)}) collective-permute-start(bf16[2,64,256]{2,1,0:T(8,128)(2,1)S(1)} %get-tuple-element.36), channel_id=1, source_target_pairs={{0,2},{1,3},{2,0},{3,1},{4,6},{5,7},{6,4},{7,5},{8,10},{9,11},{10,... | collective-permute-start | bytes 196616 | tf_op jit(solution)/shard_map/ppermute | solution.py:37
  2.9 0.4 %collective-permute-start.3 = (bf16[2,64,256]{2,1,0:T(8,128)(2,1)S(1)}, bf16[2,64,256]{2,1,0:T(8,128)(2,1)S(1)}, u32[]{:S(2)}, u32[]{:S(2)}) collective-permute-start(bf16[2,64,256]{2,1,0:T(8,128)(2,1)S(1)} %get-tuple-element.37), channel_id=1, source_target_pairs={{0,1},{1,0},{2,3},{3,2},{4,5},{5,4},{6,7},{7,6},{8,9},{9,8},{10,11... | collective-permute-start | bytes 196616 | tf_op jit(solution)/shard_map/ppermute | solution.py:37
  3.2 2.5 %collective-permute-done.5 = bf16[2,64,256]{2,1,0:T(8,128)(2,1)S(1)} collective-permute-done((bf16[2,64,256]{2,1,0:T(8,128)(2,1)S(1)}, bf16[2,64,256]{2,1,0:T(8,128)(2,1)S(1)}, u32[]{:S(2)}, u32[]{:S(2)}) %collective-permute-start.5) | collective-permute-done | bytes 65568 | tf_op jit(solution)/shard_map/ppermute | solution.py:37
  5.8 1.4 %collective-permute-done.4 = bf16[2,64,256]{2,1,0:T(8,128)(2,1)S(1)} collective-permute-done((bf16[2,64,256]{2,1,0:T(8,128)(2,1)S(1)}, bf16[2,64,256]{2,1,0:T(8,128)(2,1)S(1)}, u32[]{:S(2)}, u32[]{:S(2)}) %collective-permute-start.4) | collective-permute-done | bytes 65568 | tf_op jit(solution)/shard_map/ppermute | solution.py:37
  7.2 0.0 collective-permute-done.3
  7.2 1.6 %collective-permute-start.6 = (bf16[4,2,64,256]{3,2,1,0:T(8,128)(2,1)S(1)}, bf16[4,2,64,256]{3,2,1,0:T(8,128)(2,1)S(1)}, u32[]{:S(2)}, u32[]{:S(2)}) collective-permute-start(bf16[4,2,64,256]{3,2,1,0:T(8,128)(2,1)S(1)} %pad_maximum_fusion.1.shard_ref), channel_id=1, source_target_pairs={{0,4},{4,8},{8,12},{12,16},{16,20},{20,24},{24,28},{28,0},{1,5},{5... | collective-permute-start | bytes 786440 | tf_op jit(solution)/shard_map/ppermute | solution.py:22
  8.8 1.3 %plan.1 = (s32[1]{0:T(128)}, s32[1]{0:T(128)}, s32[3,8,128]{2,1,0:T(8,128)}) custom-call(s32[4]{0:T(128)} %docs_ref.1, s32[1]{0:T(128)} %bitcast.index_ref), custom_call_target="tpu_custom_call" | custom-call | flops 100000000 | bytes 1048576 | tf_op jit(solution)/shard_map/plan/pallas_call | solution.py:225
  10.8 1.6 %collective-permute-start.7 = (bf16[4,2,64,256]{3,2,1,0:T(8,128)(2,1)S(1)}, bf16[4,2,64,256]{3,2,1,0:T(8,128)(2,1)S(1)}, u32[]{:S(2)}, u32[]{:S(2)}) collective-permute-start(bf16[4,2,64,256]{3,2,1,0:T(8,128)(2,1)S(1)} %pad_maximum_fusion.1.shard_ref), channel_id=1, source_target_pairs={{0,8},{4,12},{8,16},{12,20},{16,24},{20,28},{24,0},{28,4},{1,9},{5... | collective-permute-start | bytes 786440 | tf_op jit(solution)/shard_map/ppermute | solution.py:22
  12.5 0.0 copy-done
  12.5 0.0 copy-start.1
  12.5 0.7 %copy-done.1 = s32[3,8,128]{2,1,0:T(8,128)S(1)} copy-done((s32[3,8,128]{2,1,0:T(8,128)S(1)}, s32[3,8,128]{2,1,0:T(8,128)}, u32[]{:S(2)}) %copy-start.1) | copy-done | bytes 12312
  13.2 1.7 %own.1 = (f32[4096,128]{1,0:T(8,128)S(1)}, f32[4096,128]{1,0:T(8,128)S(1)}, f32[4096,128]{1,0:T(8,128)S(1)}) custom-call(s32[3,8,128]{2,1,0:T(8,128)S(1)} %copy-done.1, bf16[256,16,128]{2,1,0:T(8,128)(2,1)S(1)} %copy-done, bf16[4,2,64,256]{3,2,1,0:T(8,128)(2,1)S(1)} %pad_maximum_fusion.1.shard_ref), custom_call_target="tpu_custom_call" | custom-call | flops 100000000 | bytes 1048576 | tf_op jit(solution)/shard_map/own/pallas_call | solution.py:256
  14.9 0.6 %collective-permute-done.6.refs_0_ = bf16[4,2,64,256]{3,2,1,0:T(8,128)(2,1)S(1)} collective-permute-done((bf16[4,2,64,256]{3,2,1,0:T(8,128)(2,1)S(1)}, bf16[4,2,64,256]{3,2,1,0:T(8,128)(2,1)S(1)}, u32[]{:S(2)}, u32[]{:S(2)}) %collective-permute-start.6) | collective-permute-done | bytes 262176 | tf_op jit(solution)/shard_map/ppermute | solution.py:22
  15.6 2.4 %one.1 = (f32[4096,128]{1,0:T(8,128)S(1)}, f32[4096,128]{1,0:T(8,128)S(1)}, f32[4096,128]{1,0:T(8,128)S(1)}) custom-call(s32[3,8,128]{2,1,0:T(8,128)S(1)} %copy-done.1, bf16[256,16,128]{2,1,0:T(8,128)(2,1)S(1)} %copy-done, f32[4096,128]{1,0:T(8,128)S(1)} %get-tuple-element.27.summed_in, f32[4096,128]{1,0:T(8,128)S(1)} %get-tuple-element.28.top_in, ...), custom_call_target="tpu_custom_call" | custom-call | flops 40000000000 | bytes 1048576 | tf_op jit(solution)/shard_map/one/pallas_call | solution.py:266
  18.0 5.0 %collective-permute-done.7.refs_0_ = bf16[4,2,64,256]{3,2,1,0:T(8,128)(2,1)S(1)} collective-permute-done((bf16[4,2,64,256]{3,2,1,0:T(8,128)(2,1)S(1)}, bf16[4,2,64,256]{3,2,1,0:T(8,128)(2,1)S(1)}, u32[]{:S(2)}, u32[]{:S(2)}) %collective-permute-start.7) | collective-permute-done | bytes 262176 | tf_op jit(solution)/shard_map/ppermute | solution.py:22
  23.1 1.6 %far.1 = bf16[256,16,128]{2,1,0:T(8,128)(2,1)} custom-call(s32[3,8,128]{2,1,0:T(8,128)S(1)} %copy-done.1, bf16[256,16,128]{2,1,0:T(8,128)(2,1)S(1)} %copy-done, f32[4096,128]{1,0:T(8,128)S(1)} %get-tuple-element.30.summed_in, f32[4096,128]{1,0:T(8,128)S(1)} %get-tuple-element.31.top_in, f32[4096,128]{1,0:T(8,128)S(1)} %get-tuple-element.32.total_in, ...), custom_call_target="tpu_custom_call" | custom-call | flops 100000000 | bytes 1048576 | tf_op jit(solution)/shard_map/far/pallas_call | solution.py:276
  (6 shorter events, 0.2 us)
Async XLA Ops:
  1.3 11.2 %copy-start = (bf16[256,16,128]{2,1,0:T(8,128)(2,1)S(1)}, bf16[256,16,128]{2,1,0:T(8,128)(2,1)}, u32[]{:S(2)}) copy-start(bf16[256,16,128]{2,1,0:T(8,128)(2,1)} %query_ref.5) | copy-start | bytes 3145732
  1.3 4.4 %collective-permute-start.5 = (bf16[2,64,256]{2,1,0:T(8,128)(2,1)S(1)}, bf16[2,64,256]{2,1,0:T(8,128)(2,1)S(1)}, u32[]{:S(2)}, u32[]{:S(2)}) collective-permute-start(bf16[2,64,256]{2,1,0:T(8,128)(2,1)S(1)} %get-tuple-element.35), channel_id=1, source_target_pairs={{0,3},{1,2},{2,1},{3,0},{4,7},{5,6},{6,5},{7,4},{8,11},{9,10},{10,... | collective-permute-start | bytes 196616 | tf_op jit(solution)/shard_map/ppermute | solution.py:37
  1.4 5.8 %collective-permute-start.4 = (bf16[2,64,256]{2,1,0:T(8,128)(2,1)S(1)}, bf16[2,64,256]{2,1,0:T(8,128)(2,1)S(1)}, u32[]{:S(2)}, u32[]{:S(2)}) collective-permute-start(bf16[2,64,256]{2,1,0:T(8,128)(2,1)S(1)} %get-tuple-element.36), channel_id=1, source_target_pairs={{0,2},{1,3},{2,0},{3,1},{4,6},{5,7},{6,4},{7,5},{8,10},{9,11},{10,... | collective-permute-start | bytes 196616 | tf_op jit(solution)/shard_map/ppermute | solution.py:37
  2.9 4.3 %collective-permute-start.3 = (bf16[2,64,256]{2,1,0:T(8,128)(2,1)S(1)}, bf16[2,64,256]{2,1,0:T(8,128)(2,1)S(1)}, u32[]{:S(2)}, u32[]{:S(2)}) collective-permute-start(bf16[2,64,256]{2,1,0:T(8,128)(2,1)S(1)} %get-tuple-element.37), channel_id=1, source_target_pairs={{0,1},{1,0},{2,3},{3,2},{4,5},{5,4},{6,7},{7,6},{8,9},{9,8},{10,11... | collective-permute-start | bytes 196616 | tf_op jit(solution)/shard_map/ppermute | solution.py:37
  7.2 8.4 %collective-permute-start.6 = (bf16[4,2,64,256]{3,2,1,0:T(8,128)(2,1)S(1)}, bf16[4,2,64,256]{3,2,1,0:T(8,128)(2,1)S(1)}, u32[]{:S(2)}, u32[]{:S(2)}) collective-permute-start(bf16[4,2,64,256]{3,2,1,0:T(8,128)(2,1)S(1)} %pad_maximum_fusion.1.shard_ref), channel_id=1, source_target_pairs={{0,4},{4,8},{8,12},{12,16},{16,20},{20,24},{24,28},{28,0},{1,5},{5... | collective-permute-start | bytes 786440 | tf_op jit(solution)/shard_map/ppermute | solution.py:22
  10.8 12.3 %collective-permute-start.7 = (bf16[4,2,64,256]{3,2,1,0:T(8,128)(2,1)S(1)}, bf16[4,2,64,256]{3,2,1,0:T(8,128)(2,1)S(1)}, u32[]{:S(2)}, u32[]{:S(2)}) collective-permute-start(bf16[4,2,64,256]{3,2,1,0:T(8,128)(2,1)S(1)} %pad_maximum_fusion.1.shard_ref), channel_id=1, source_target_pairs={{0,8},{4,12},{8,16},{12,20},{16,24},{20,28},{24,0},{28,4},{1,9},{5... | collective-permute-start | bytes 786440 | tf_op jit(solution)/shard_map/ppermute | solution.py:22
  12.5 0.7 %copy-start.1 = (s32[3,8,128]{2,1,0:T(8,128)S(1)}, s32[3,8,128]{2,1,0:T(8,128)}, u32[]{:S(2)}) copy-start(s32[3,8,128]{2,1,0:T(8,128)} %get-tuple-element.24.behind_ref) | copy-start | bytes 36868

commit v2 on v1

--- a/solution.py
+++ b/solution.py
@@ -14,28 +14,19 @@
 lowest = -1e30
 
 
-def passed_along(shard, axis, by, parity=None):
-    size = lax.axis_size(axis)
-    pairs = [(i, (i + by) % size) for i in range(size)]
-    if parity is not None:
-        pairs = [(i, far if i % 2 == parity else i ^ 1) for i, far in pairs]
-    return lax.ppermute(shard, axis, pairs)
-
-
-def exchanged(pieces, axis):
-    size = lax.axis_size(axis)
-    me = lax.axis_index(axis)
-    bits = size.bit_length() - 1
-    shape = pieces.shape
-    pieces = pieces.reshape(*[2] * bits, *shape[1:])
-    for bit in range(bits):
-        flipped = jnp.flip(pieces, bits - 1 - bit)
-        pieces = jnp.where((me >> bit) & 1 == 1, flipped, pieces)
-    pieces = pieces.reshape(shape)
-    held = [pieces[0]]
-    for other in range(1, size):
-        held.append(lax.ppermute(pieces[other], axis, [(i, i ^ other) for i in range(size)]))
-    return jnp.stack(held)
+def passed_along(piece, by, across=0, parity=None):
+    shards, parts = lax.axis_size("ctx"), lax.axis_size("kvh")
+    pairs = []
+    for shard in range(shards):
+        to = (shard + by) % shards if parity is None or shard % 2 == parity else shard ^ 1
+        pairs += [(shard * parts + part, to * parts + (part ^ across)) for part in range(parts)]
+    return lax.ppermute(piece, ("ctx", "kvh"), pairs)
+
+
+def for_groups(pieces, me):
+    pieces = pieces.reshape(2, 2, *pieces.shape[1:])
+    pieces = jnp.where(me & 1 == 1, jnp.flip(pieces, 1), pieces)
+    return jnp.where(me >> 1 == 1, jnp.flip(pieces, 0), pieces)
 
 
 def plan_kernel(parts, longest, docs_ref, index_ref, spans_ref, last_ref, behind_ref):
@@ -60,21 +51,23 @@
 
 
 def fill(me, shard_refs, key_win, value_win):
+    core, side = me & 1, me >> 1
     at = 0
-    for ref in reversed(shard_refs):
-        pieces, count, tokens, depth = ref.shape
-        depth = depth // 2
-        group = BLOCK // tokens
-        for piece in range(0, pieces, group):
+    for refs in reversed(shard_refs):
+        for apart, ref in enumerate(refs):
+            _, count, _, depth = ref.shape
+            depth = depth // 2
+            block = (side ^ apart) if len(refs) > 1 else 0
+            rows = pl.ds(pl.multiple_of(at + block * BLOCK, BLOCK), BLOCK)
             for head in range(count):
                 lanes = slice(head * depth, (head + 1) * depth)
                 key, value = (
-                    jnp.concatenate([ref[((piece + i) ^ me) % pieces, head, :, half] for i in range(group)], axis=0)
+                    jnp.concatenate([ref[i ^ core, head, :, half] for i in range(2)], axis=0)
                     for half in (slice(0, depth), slice(depth, 2 * depth))
                 )
-                key_win[lanes, at : at + BLOCK] = key.T
-                value_win[at : at + BLOCK, lanes] = value
-            at += BLOCK
+                key_win[lanes, rows] = key.T
+                value_win[rows, lanes] = value
+        at += BLOCK * len(refs)
 
 
 def key_scores(count, heads, query, keys):
@@ -113,12 +106,13 @@
         lax.fori_loop(0, steps // TOGETHER, together, None)
 
 
-def own_kernel(scale, behind_ref, query_ref, shard_ref, summed_ref, top_ref, total_ref, key_win, value_win):
+def own_kernel(scale, behind_ref, query_ref, *refs):
+    *shard_refs, summed_ref, top_ref, total_ref, key_win, value_win = refs
     rows, heads, depth = query_ref.shape
-    count = shard_ref.shape[1]
+    count = shard_refs[0].shape[1]
     blocks = rows // BLOCK
     *behind, me = [jnp.max(behind_ref[row]) for row in range(blocks + 1)]
-    fill(me, [shard_ref], key_win, value_win)
+    fill(me, [shard_refs], key_win, value_win)
     chunk_rows = CHUNK * heads
     ahead = lax.broadcasted_iota(jnp.int32, (chunk_rows, BLOCK), 1)
     ahead = ahead - lax.broadcasted_iota(jnp.int32, (chunk_rows, BLOCK), 0) // heads
@@ -154,11 +148,12 @@
         shard_refs, (*out_refs, key_win, value_win) = refs[: -outs - 2], refs[-outs - 2 :]
     rows, heads, depth = query_ref.shape
     count = shard_refs[0].shape[1]
+    groups = [shard_refs[i : i + 2] for i in range(0, len(shard_refs), 2)]
     blocks = rows // BLOCK
     window = value_win.shape[0] // BLOCK
     *behind, me = [jnp.max(behind_ref[row]) for row in range(blocks + 1)]
     fars = [jnp.clip(behind[block] - offset - block, 0, window) for block in range(blocks)]
-    fill(me, shard_refs, key_win, value_win)
+    fill(me, groups, key_win, value_win)
     chunk_rows = CHUNK * heads
     rate = scale * math.log2(math.e)
 
@@ -216,33 +211,37 @@
     smem, vmem = pl.BlockSpec(memory_space=pltpu.SMEM), pl.BlockSpec(memory_space=pltpu.VMEM)
     params = pltpu.CompilerParams(vmem_limit_bytes=24 * 1024 * 1024)
     scale = 1.0 / math.sqrt(depth)
-    light, heavy = (
-        pl.CostEstimate(flops=flops, bytes_accessed=2**20, transcendentals=10**6) for flops in (10**8, 4 * 10**10)
+    light, medium = (
+        pl.CostEstimate(flops=flops, bytes_accessed=2**20, transcendentals=10**6) for flops in (10**8, 10**9)
     )
     shape = jax.ShapeDtypeStruct
     me = lax.axis_index("kvh")
     index = (lax.axis_index("ctx") * parts + me).astype(jnp.int32).reshape(1)
     spans, last, nearer = pl.pallas_call(
         functools.partial(plan_kernel, parts, behind),
+        cost_estimate=medium,
         out_shape=(shape((1,), jnp.int32), shape((1,), jnp.int32), shape((per_shard + 1, 8, 128), jnp.int32)),
         in_specs=[smem] * 2,
         out_specs=(smem, smem, vmem),
-        cost_estimate=light,
         name="plan",
     )(doc_blocks, index)
     both = lax.optimization_barrier(jnp.concatenate([keys, values], axis=2))
     both = both.reshape(tokens, parts, count, 2 * depth).transpose(1, 2, 0, 3)
-    own = exchanged(both, "kvh")
-    far = [passed_along(own, "ctx", 2)]
-    one = passed_along(own, "ctx", 1)
+    pieces = for_groups(both, me)
+    swapped = passed_along(pieces[:, 1], 0, across=1)
+    here, there = (jnp.stack([pieces[side, 0], swapped[side]]) for side in range(2))
+    own = [here, passed_along(there, 0, across=2)]
+    far = [passed_along(here, 2), passed_along(there, 2, across=2)]
+    one = [passed_along(here, 1), passed_along(there, 1, across=2)]
     for distance in range(3, behind):
-        send = functools.partial(passed_along, axis="ctx", by=distance)
-        far.append(lax.cond(spans[0] >= distance, send, lambda x: x, own))
-    half = parts // 2
-    sent = jnp.where(me >= half, own[:half], own[half:])
-    sends = [functools.partial(passed_along, axis="ctx", by=behind, parity=parity) for parity in (0, 1, None)]
-    far.append(lax.switch(last[0], [lambda x: x, *sends], sent))
-    own, far[1:] = lax.optimization_barrier((own, far[1:]))
+        send = functools.partial(passed_along, by=distance)
+        far += [lax.cond(spans[0] >= distance, send, lambda x: x, x) for x in own]
+
+    def late(parity):
+        return lambda *halves: passed_along(jnp.where(me >= parts // 2, *halves), behind, parity=parity)
+
+    far.append(lax.switch(last[0], [lambda *halves: halves[0], late(0), late(1), late(None)], *own))
+    own, far[2:] = lax.optimization_barrier((own, far[2:]))
 
     state = [shape((rows * heads, depth), jnp.float32)] * 3
 
@@ -256,23 +255,23 @@
     kept = pl.pallas_call(
         functools.partial(own_kernel, scale),
         out_shape=state,
-        in_specs=[vmem] * 3,
+        in_specs=[vmem] * 4,
         out_specs=[vmem] * 3,
-        scratch_shapes=window([own]),
+        scratch_shapes=window(own),
         compiler_params=params,
         cost_estimate=light,
         name="own",
-    )(nearer, queries, own)
+    )(nearer, queries, *own)
     kept = pl.pallas_call(
         functools.partial(join_kernel, scale, 0, False),
         out_shape=state,
-        in_specs=[vmem] * 6,
+        in_specs=[vmem] * 7,
         out_specs=[vmem] * 3,
-        scratch_shapes=window([one]),
+        scratch_shapes=window(one),
         compiler_params=params,
-        cost_estimate=heavy,
+        cost_estimate=light,
         name="one",
-    )(nearer, queries, *kept, one)
+    )(nearer, queries, *kept, *one)
     return pl.pallas_call(
         functools.partial(join_kernel, scale, per_shard, True),
         out_shape=shape(queries.shape, queries.dtype),

time: 25.2 us -> 22.8 us (0.905)
  waiting for transfers between devices: 9.61 us -> 3.11 us
  starting transfers between devices: 5.15 us -> 7.79 us
  Pallas kernels: 7.07 us -> 8.13 us
  local copies, waits for them, and re-layouts: 0.88 us -> 1.45 us
    ppermute x5 -> x6, waiting for transfers between devices: 9.61 us -> 3.11 us  [passed_along(): return lax.ppermute(piece, ('ctx', 'kvh'), pairs)]
    ppermute x5 -> x6, starting transfers between devices: 5.15 us -> 7.79 us  [passed_along(): return lax.ppermute(piece, ('ctx', 'kvh'), pairs)]
    pallas_call x1, Pallas kernels: 1.58 us -> 2.49 us  [body(): pl.pallas_call(functools.partial(join_kernel, scale, per_shard, True), ou...]
    cond x0 -> x1, local copies, waits for them, and re-layouts: none -> 0.65 us
  transfers between devices with their start and end apart: 5 -> 6, of which waited for: 4 -> 2; matrix products, arithmetic and copies ran while one was open for 0% -> 3% of each run, Pallas kernels for 22% -> 25%
where the time goes in v2:
time: 22.8 us; the launch traced here: 22.4 us
  Pallas kernels  8.13 us (36%)
  starting transfers between devices  7.79 us (34%)
  waiting for transfers between devices  3.11 us (14%)
  local copies, waits for them, and re-layouts  1.45 us (6%)
  other arithmetic  1.13 us (5%)
  between operations  0.83 us (4%)
    ppermute x6, starting transfers between devices, passed_along(): return lax.ppermute(piece, ('ctx', 'kvh'), pairs)  7.79 us
    ppermute x6, waiting for transfers between devices, passed_along(): return lax.ppermute(piece, ('ctx', 'kvh'), pairs)  3.11 us
    pallas_call x1, Pallas kernels, body(): pl.pallas_call(functools.partial(join_kernel, scale, per_shard, True), ou...  2.49 us
    pallas_call x1, Pallas kernels, body(): pl.pallas_call(functools.partial(join_kernel, scale, 0, False), out_shape...  2.45 us
    pallas_call x1, Pallas kernels, body(): pl.pallas_call(functools.partial(own_kernel, scale), out_shape=state, in_...  1.75 us
    pallas_call x1, Pallas kernels, body(): pl.pallas_call(functools.partial(plan_kernel, parts, behind), cost_estima...  1.44 us
    concatenate x1, other arithmetic, body(): both = lax.optimization_barrier(jnp.concatenate([keys, values], axis=2))  1 us
    unnamed x4, local copies, waits for them, and re-layouts  0.71 us
  transfers between devices with their start and end apart: 6, of which 2 were waited for; matrix products, arithmetic and copies ran while one was open for 3% of the time, Pallas kernels for 25%

profile of v2, /device:TPU:6, one launch (start us, length us, event | category | flops | bytes accessed | tf_op | source)
XLA Modules:
  0.0 22.4 jit_solution(12281061200971925208)
XLA Ops:
  0.0 1.0 %pad_maximum_fusion = bf16[64,8,256]{2,1,0:T(8,128)(2,1)S(1)} fusion(bf16[64,8,128]{2,1,0:T(8,128)(2,1)} %param.10, bf16[64,8,128]{2,1,0:T(8,128)(2,1)} %param.9), kind=kLoop, calls=%fused_computation.5 | loop fusion | flops 524288 | bytes 524288 | tf_op jit(solution)/shard_map/concatenate | solution.py:228
  1.1 0.1 reverse_select_fusion.1
  1.1 0.1 reverse_select_fusion
  1.2 0.1 collective-permute-start.3
  1.3 1.3 %collective-permute-done.3 = bf16[2,2,64,256]{3,2,1,0:T(8,128)(2,1)S(1)} collective-permute-done((bf16[2,2,64,256]{3,2,1,0:T(8,128)(2,1)S(1)}, bf16[2,2,64,256]{3,2,1,0:T(8,128)(2,1)S(1)}, u32[]{:S(2)}, u32[]{:S(2)}) %collective-permute-start.3) | collective-permute-done | bytes 131104 | tf_op jit(solution)/shard_map/ppermute | solution.py:23
  2.6 0.6 %collective-permute-start.4 = (bf16[2,2,64,256]{3,2,1,0:T(8,128)(2,1)S(1)}, bf16[2,2,64,256]{3,2,1,0:T(8,128)(2,1)S(1)}, u32[]{:S(2)}, u32[]{:S(2)}) collective-permute-start(bf16[2,2,64,256]{3,2,1,0:T(8,128)(2,1)S(1)} %pad_maximum_fusion.2), channel_id=1, source_target_pairs={{0,2},{1,3},{2,0},{3,1},{4,6},{5,7},{6,4},{7,5},{8,10},{9,11},{10,... | collective-permute-start | bytes 393224 | tf_op jit(solution)/shard_map/ppermute | solution.py:23
  3.2 1.6 %collective-permute-start.5 = (bf16[2,2,64,256]{3,2,1,0:T(8,128)(2,1)S(1)}, bf16[2,2,64,256]{3,2,1,0:T(8,128)(2,1)S(1)}, u32[]{:S(2)}, u32[]{:S(2)}) collective-permute-start(bf16[2,2,64,256]{3,2,1,0:T(8,128)(2,1)S(1)} %pad_maximum_fusion.1.refs_0_), channel_id=1, source_target_pairs={{0,4},{1,5},{2,6},{3,7},{4,8},{5,9},{6,10},{7,11},{8,12},{9,13},{1... | collective-permute-start | bytes 393224 | tf_op jit(solution)/shard_map/ppermute | solution.py:23
  4.8 2.4 %collective-permute-start.6 = (bf16[2,2,64,256]{3,2,1,0:T(8,128)(2,1)S(1)}, bf16[2,2,64,256]{3,2,1,0:T(8,128)(2,1)S(1)}, u32[]{:S(2)}, u32[]{:S(2)}) collective-permute-start(bf16[2,2,64,256]{3,2,1,0:T(8,128)(2,1)S(1)} %pad_maximum_fusion.2), channel_id=1, source_target_pairs={{0,6},{1,7},{2,4},{3,5},{4,10},{5,11},{6,8},{7,9},{8,14},{9,15},{1... | collective-permute-start | bytes 393224 | tf_op jit(solution)/shard_map/ppermute | solution.py:23
  7.3 1.6 %collective-permute-start.7 = (bf16[2,2,64,256]{3,2,1,0:T(8,128)(2,1)S(1)}, bf16[2,2,64,256]{3,2,1,0:T(8,128)(2,1)S(1)}, u32[]{:S(2)}, u32[]{:S(2)}) collective-permute-start(bf16[2,2,64,256]{3,2,1,0:T(8,128)(2,1)S(1)} %pad_maximum_fusion.1.refs_0_), channel_id=1, source_target_pairs={{0,8},{1,9},{2,10},{3,11},{4,12},{5,13},{6,14},{7,15},{8,16},{9,17... | collective-permute-start | bytes 393224 | tf_op jit(solution)/shard_map/ppermute | solution.py:23
  8.9 1.5 %collective-permute-start.8 = (bf16[2,2,64,256]{3,2,1,0:T(8,128)(2,1)S(1)}, bf16[2,2,64,256]{3,2,1,0:T(8,128)(2,1)S(1)}, u32[]{:S(2)}, u32[]{:S(2)}) collective-permute-start(bf16[2,2,64,256]{3,2,1,0:T(8,128)(2,1)S(1)} %pad_maximum_fusion.2), channel_id=1, source_target_pairs={{0,10},{1,11},{2,8},{3,9},{4,14},{5,15},{6,12},{7,13},{8,18},{9,19... | collective-permute-start | bytes 393224 | tf_op jit(solution)/shard_map/ppermute | solution.py:23
  10.4 0.0 copy-start
  10.4 1.4 %plan.1 = (s32[1]{0:T(128)}, s32[1]{0:T(128)}, s32[3,8,128]{2,1,0:T(8,128)}) custom-call(s32[4]{0:T(128)} %docs_ref.1, s32[1]{0:T(128)} %bitcast.index_ref), custom_call_target="tpu_custom_call" | custom-call | flops 1000000000 | bytes 1048576 | tf_op jit(solution)/shard_map/plan/pallas_call | solution.py:220
  12.4 0.0 collective-permute-done.4.refs_1_
  12.4 0.7 %conditional.1 = (bf16[2,2,64,256]{3,2,1,0:T(8,128)(2,1)}) conditional(s32[]{:T(128)} %bitcast.7, bf16[2,2,64,256]{3,2,1,0:T(8,128)(2,1)S(1)} %pad_maximum_fusion.1.refs_0_, (s32[]{:T(128)}, bf16[2,2,64,256]{3,2,1,0:T(8,128)(2,1)S(1)}, bf16[2,2,64,256]{3,2,1,0:T(8,128)(2,1)S(1)}) %tuple.18, (s32[]{:T(128)}, ...), branch_computations={%region_0.1_spmd, %region_1.2_spmd, %region_2.3_spmd, %region_3.4_... | conditional | flops 65537 | bytes 917562 | solution.py:243
  12.4 0.7 %copy.7 = bf16[2,2,64,256]{3,2,1,0:T(8,128)(2,1)} copy(bf16[2,2,64,256]{3,2,1,0:T(8,128)(2,1)S(1)} %param) | data formatting | bytes 262144 | tf_op jit(solution)/shard_map/cond
  13.1 0.0 copy-done
  13.1 0.0 copy-start.1
  13.1 0.7 %copy-done.1 = s32[3,8,128]{2,1,0:T(8,128)S(1)} copy-done((s32[3,8,128]{2,1,0:T(8,128)S(1)}, s32[3,8,128]{2,1,0:T(8,128)}, u32[]{:S(2)}) %copy-start.1) | copy-done | bytes 12312
  13.8 1.8 %own.1 = (f32[4096,128]{1,0:T(8,128)S(1)}, f32[4096,128]{1,0:T(8,128)S(1)}, f32[4096,128]{1,0:T(8,128)S(1)}) custom-call(s32[3,8,128]{2,1,0:T(8,128)S(1)} %copy-done.1, bf16[256,16,128]{2,1,0:T(8,128)(2,1)S(1)} %copy-done, bf16[2,2,64,256]{3,2,1,0:T(8,128)(2,1)S(1)} %pad_maximum_fusion.1.refs_0_, bf16[2,2,64,256]{3,2,1,0:T(8,128)(2,1)S(1)} %collective-permute-done.4.refs_1_), custom_call_target="tpu_custom_call" | custom-call | flops 100000000 | bytes 1048576 | tf_op jit(solution)/shard_map/own/pallas_call | solution.py:255
  15.5 0.0 collective-permute-done.5.refs_0_
  15.5 0.0 collective-permute-done.6.refs_1_
  15.6 2.4 %one.1 = (f32[4096,128]{1,0:T(8,128)S(1)}, f32[4096,128]{1,0:T(8,128)S(1)}, f32[4096,128]{1,0:T(8,128)S(1)}) custom-call(s32[3,8,128]{2,1,0:T(8,128)S(1)} %copy-done.1, bf16[256,16,128]{2,1,0:T(8,128)(2,1)S(1)} %copy-done, f32[4096,128]{1,0:T(8,128)S(1)} %get-tuple-element.53.summed_in, f32[4096,128]{1,0:T(8,128)S(1)} %get-tuple-element.54.top_in, ...), custom_call_target="tpu_custom_call" | custom-call | flops 100000000 | bytes 1048576 | tf_op jit(solution)/shard_map/one/pallas_call | solution.py:265
  18.0 0.0 collective-permute-done.7.refs_0_
  18.0 1.8 %collective-permute-done.8.refs_1_ = bf16[2,2,64,256]{3,2,1,0:T(8,128)(2,1)S(1)} collective-permute-done((bf16[2,2,64,256]{3,2,1,0:T(8,128)(2,1)S(1)}, bf16[2,2,64,256]{3,2,1,0:T(8,128)(2,1)S(1)}, u32[]{:S(2)}, u32[]{:S(2)}) %collective-permute-start.8) | collective-permute-done | bytes 131104 | tf_op jit(solution)/shard_map/ppermute | solution.py:23
  19.8 2.5 %far.1 = bf16[256,16,128]{2,1,0:T(8,128)(2,1)} custom-call(s32[3,8,128]{2,1,0:T(8,128)S(1)} %copy-done.1, bf16[256,16,128]{2,1,0:T(8,128)(2,1)S(1)} %copy-done, f32[4096,128]{1,0:T(8,128)S(1)} %get-tuple-element.56.summed_in, f32[4096,128]{1,0:T(8,128)S(1)} %get-tuple-element.57.top_in, f32[4096,128]{1,0:T(8,128)S(1)} %get-tuple-element.58.total_in, ...), custom_call_target="tpu_custom_call" | custom-call | flops 100000000 | bytes 1048576 | tf_op jit(solution)/shard_map/far/pallas_call | solution.py:275
  (6 shorter events, 0.1 us)
Async XLA Ops:
  1.2 1.4 %collective-permute-start.3 = (bf16[2,2,64,256]{3,2,1,0:T(8,128)(2,1)S(1)}, bf16[2,2,64,256]{3,2,1,0:T(8,128)(2,1)S(1)}, u32[]{:S(2)}, u32[]{:S(2)}) collective-permute-start(bf16[2,2,64,256]{3,2,1,0:T(8,128)(2,1)S(1)} %slice_bitcast_fusion), channel_id=1, source_target_pairs={{0,1},{1,0},{2,3},{3,2},{4,5},{5,4},{6,7},{7,6},{8,9},{9,8},{10,11... | collective-permute-start | bytes 393224 | tf_op jit(solution)/shard_map/ppermute | solution.py:23
  2.6 9.7 %collective-permute-start.4 = (bf16[2,2,64,256]{3,2,1,0:T(8,128)(2,1)S(1)}, bf16[2,2,64,256]{3,2,1,0:T(8,128)(2,1)S(1)}, u32[]{:S(2)}, u32[]{:S(2)}) collective-permute-start(bf16[2,2,64,256]{3,2,1,0:T(8,128)(2,1)S(1)} %pad_maximum_fusion.2), channel_id=1, source_target_pairs={{0,2},{1,3},{2,0},{3,1},{4,6},{5,7},{6,4},{7,5},{8,10},{9,11},{10,... | collective-permute-start | bytes 393224 | tf_op jit(solution)/shard_map/ppermute | solution.py:23
  3.2 12.3 %collective-permute-start.5 = (bf16[2,2,64,256]{3,2,1,0:T(8,128)(2,1)S(1)}, bf16[2,2,64,256]{3,2,1,0:T(8,128)(2,1)S(1)}, u32[]{:S(2)}, u32[]{:S(2)}) collective-permute-start(bf16[2,2,64,256]{3,2,1,0:T(8,128)(2,1)S(1)} %pad_maximum_fusion.1.refs_0_), channel_id=1, source_target_pairs={{0,4},{1,5},{2,6},{3,7},{4,8},{5,9},{6,10},{7,11},{8,12},{9,13},{1... | collective-permute-start | bytes 393224 | tf_op jit(solution)/shard_map/ppermute | solution.py:23
  4.8 10.7 %collective-permute-start.6 = (bf16[2,2,64,256]{3,2,1,0:T(8,128)(2,1)S(1)}, bf16[2,2,64,256]{3,2,1,0:T(8,128)(2,1)S(1)}, u32[]{:S(2)}, u32[]{:S(2)}) collective-permute-start(bf16[2,2,64,256]{3,2,1,0:T(8,128)(2,1)S(1)} %pad_maximum_fusion.2), channel_id=1, source_target_pairs={{0,6},{1,7},{2,4},{3,5},{4,10},{5,11},{6,8},{7,9},{8,14},{9,15},{1... | collective-permute-start | bytes 393224 | tf_op jit(solution)/shard_map/ppermute | solution.py:23
  7.3 10.7 %collective-permute-start.7 = (bf16[2,2,64,256]{3,2,1,0:T(8,128)(2,1)S(1)}, bf16[2,2,64,256]{3,2,1,0:T(8,128)(2,1)S(1)}, u32[]{:S(2)}, u32[]{:S(2)}) collective-permute-start(bf16[2,2,64,256]{3,2,1,0:T(8,128)(2,1)S(1)} %pad_maximum_fusion.1.refs_0_), channel_id=1, source_target_pairs={{0,8},{1,9},{2,10},{3,11},{4,12},{5,13},{6,14},{7,15},{8,16},{9,17... | collective-permute-start | bytes 393224 | tf_op jit(solution)/shard_map/ppermute | solution.py:23
  8.9 10.9 %collective-permute-start.8 = (bf16[2,2,64,256]{3,2,1,0:T(8,128)(2,1)S(1)}, bf16[2,2,64,256]{3,2,1,0:T(8,128)(2,1)S(1)}, u32[]{:S(2)}, u32[]{:S(2)}) collective-permute-start(bf16[2,2,64,256]{3,2,1,0:T(8,128)(2,1)S(1)} %pad_maximum_fusion.2), channel_id=1, source_target_pairs={{0,10},{1,11},{2,8},{3,9},{4,14},{5,15},{6,12},{7,13},{8,18},{9,19... | collective-permute-start | bytes 393224 | tf_op jit(solution)/shard_map/ppermute | solution.py:23
  10.4 2.7 %copy-start = (bf16[256,16,128]{2,1,0:T(8,128)(2,1)S(1)}, bf16[256,16,128]{2,1,0:T(8,128)(2,1)}, u32[]{:S(2)}) copy-start(bf16[256,16,128]{2,1,0:T(8,128)(2,1)} %query_ref.5) | copy-start | bytes 3145732
  13.1 0.7 %copy-start.1 = (s32[3,8,128]{2,1,0:T(8,128)S(1)}, s32[3,8,128]{2,1,0:T(8,128)}, u32[]{:S(2)}) copy-start(s32[3,8,128]{2,1,0:T(8,128)} %get-tuple-element.49.behind_ref) | copy-start | bytes 36868

commit v3 on v2

--- a/solution.py
+++ b/solution.py
@@ -50,10 +50,11 @@
         behind_ref[row] = jnp.full(behind_ref.shape[1:], number, jnp.int32)
 
 
-def fill(me, shard_refs, key_win, value_win):
+def fill(me, shard_refs, key_win, value_win, nearer=0):
     core, side = me & 1, me >> 1
-    at = 0
-    for refs in reversed(shard_refs):
+    at = value_win.shape[0] - nearer * BLOCK
+    for refs in shard_refs:
+        at -= BLOCK * len(refs)
         for apart, ref in enumerate(refs):
             _, count, _, depth = ref.shape
             depth = depth // 2
@@ -67,7 +68,6 @@
                 )
                 key_win[lanes, rows] = key.T
                 value_win[rows, lanes] = value
-        at += BLOCK * len(refs)
 
 
 def key_scores(count, heads, query, keys):
@@ -143,7 +143,9 @@
 def join_kernel(scale, offset, final, behind_ref, query_ref, summed_in, top_in, total_in, *refs):
     outs = 1 if final else 3
     if final:
-        *shard_refs, out_to, key_win, value_win, out_ref, left = refs
+        extra = (len(refs) - 8) // 2
+        shard_refs, rare_refs, refs = refs[:2], refs[2 : 2 + extra], refs[2 + extra :]
+        out_to, key_win, value_win, out_ref, left, landed, *landing = refs
     else:
         shard_refs, (*out_refs, key_win, value_win) = refs[: -outs - 2], refs[-outs - 2 :]
     rows, heads, depth = query_ref.shape
@@ -154,6 +156,20 @@
     *behind, me = [jnp.max(behind_ref[row]) for row in range(blocks + 1)]
     fars = [jnp.clip(behind[block] - offset - block, 0, window) for block in range(blocks)]
     fill(me, groups, key_win, value_win)
+    if final:
+
+        @pl.when(jnp.maximum(*fars) > 2)
+        def _():
+            copies = [
+                pltpu.make_async_copy(ref, to, landed.at[i]) for i, (ref, to) in enumerate(zip(rare_refs, landing))
+            ]
+            for copy in copies:
+                copy.start()
+            for copy in copies:
+                copy.wait()
+            rare = [landing[i : i + 2] for i in range(0, extra, 2)]
+            fill(me, rare, key_win, value_win, 2)
+
     chunk_rows = CHUNK * heads
     rate = scale * math.log2(math.e)
 
@@ -275,9 +291,15 @@
     return pl.pallas_call(
         functools.partial(join_kernel, scale, per_shard, True),
         out_shape=shape(queries.shape, queries.dtype),
-        in_specs=[vmem] * (5 + len(far)),
+        in_specs=[vmem] * 7 + [pl.BlockSpec(memory_space=pl.ANY)] * (len(far) - 2),
         out_specs=pl.BlockSpec(memory_space=pl.ANY),
-        scratch_shapes=window(far) + [pltpu.VMEM(queries.shape, queries.dtype), pltpu.SemaphoreType.DMA],
+        scratch_shapes=[
+            *window(far),
+            pltpu.VMEM(queries.shape, queries.dtype),
+            pltpu.SemaphoreType.DMA,
+            pltpu.SemaphoreType.DMA((len(far) - 2,)),
+            *[pltpu.VMEM(piece.shape, piece.dtype) for piece in far[2:]],
+        ],
         compiler_params=params,
         cost_estimate=light,
         name="far",

time: 22.8 us -> 21.9 us (0.961)
  Pallas kernels: 8.13 us -> 5.5 us
  waiting for transfers between devices: 3.11 us -> 4.85 us
    ppermute x6, waiting for transfers between devices: 3.11 us -> 4.85 us  [passed_along(): return lax.ppermute(piece, ('ctx', 'kvh'), pairs)]
    pallas_call x1, Pallas kernels: 2.45 us -> 0.72 us  [body(): pl.pallas_call(functools.partial(join_kernel, scale, 0, False), out_shape...]
    pallas_call x1, Pallas kernels: 2.49 us -> 1.58 us  [body(): pl.pallas_call(functools.partial(join_kernel, scale, per_shard, True), ou...]
  transfers between devices with their start and end apart: 6 -> 6, of which waited for: 2 -> 3; matrix products, arithmetic and copies ran while one was open for 3% -> 3% of each run, Pallas kernels for 25% -> 18%
where the time goes in v3:
time: 21.9 us; the launch traced here: 21.5 us
  starting transfers between devices  7.79 us (36%)
  Pallas kernels  5.5 us (25%)
  waiting for transfers between devices  4.85 us (22%)
  local copies, waits for them, and re-layouts  1.45 us (7%)
  other arithmetic  1.13 us (5%)
  between operations  0.82 us (4%)
    ppermute x6, starting transfers between devices, passed_along(): return lax.ppermute(piece, ('ctx', 'kvh'), pairs)  7.79 us
    ppermute x6, waiting for transfers between devices, passed_along(): return lax.ppermute(piece, ('ctx', 'kvh'), pairs)  4.85 us
    pallas_call x1, Pallas kernels, body(): pl.pallas_call(functools.partial(own_kernel, scale), out_shape=state, in_...  1.75 us
    pallas_call x1, Pallas kernels, body(): pl.pallas_call(functools.partial(join_kernel, scale, per_shard, True), ou...  1.58 us
    pallas_call x1, Pallas kernels, body(): pl.pallas_call(functools.partial(plan_kernel, parts, behind), cost_estima...  1.44 us
    concatenate x1, other arithmetic, body(): both = lax.optimization_barrier(jnp.concatenate([keys, values], axis=2))  1 us
    pallas_call x1, Pallas kernels, body(): pl.pallas_call(functools.partial(join_kernel, scale, 0, False), out_shape...  0.72 us
    unnamed x4, local copies, waits for them, and re-layouts  0.71 us
  transfers between devices with their start and end apart: 6, of which 3 were waited for; matrix products, arithmetic and copies ran while one was open for 3% of the time, Pallas kernels for 18%

profile of v3, /device:TPU:6, one launch (start us, length us, event | category | flops | bytes accessed | tf_op | source)
XLA Modules:
  0.0 21.5 jit_solution(2647648803694883375)
XLA Ops:
  0.0 1.0 %pad_maximum_fusion = bf16[64,8,256]{2,1,0:T(8,128)(2,1)S(1)} fusion(bf16[64,8,128]{2,1,0:T(8,128)(2,1)} %param.10, bf16[64,8,128]{2,1,0:T(8,128)(2,1)} %param.9), kind=kLoop, calls=%fused_computation.5 | loop fusion | flops 524288 | bytes 524288 | tf_op jit(solution)/shard_map/concatenate | solution.py:244
  1.1 0.1 reverse_select_fusion.1
  1.1 0.1 reverse_select_fusion
  1.2 0.1 collective-permute-start.3
  1.3 1.3 %collective-permute-done.3 = bf16[2,2,64,256]{3,2,1,0:T(8,128)(2,1)S(1)} collective-permute-done((bf16[2,2,64,256]{3,2,1,0:T(8,128)(2,1)S(1)}, bf16[2,2,64,256]{3,2,1,0:T(8,128)(2,1)S(1)}, u32[]{:S(2)}, u32[]{:S(2)}) %collective-permute-start.3) | collective-permute-done | bytes 131104 | tf_op jit(solution)/shard_map/ppermute | solution.py:23
  2.6 0.6 %collective-permute-start.4 = (bf16[2,2,64,256]{3,2,1,0:T(8,128)(2,1)S(1)}, bf16[2,2,64,256]{3,2,1,0:T(8,128)(2,1)S(1)}, u32[]{:S(2)}, u32[]{:S(2)}) collective-permute-start(bf16[2,2,64,256]{3,2,1,0:T(8,128)(2,1)S(1)} %pad_maximum_fusion.2), channel_id=1, source_target_pairs={{0,2},{1,3},{2,0},{3,1},{4,6},{5,7},{6,4},{7,5},{8,10},{9,11},{10,... | collective-permute-start | bytes 393224 | tf_op jit(solution)/shard_map/ppermute | solution.py:23
  3.2 1.6 %collective-permute-start.5 = (bf16[2,2,64,256]{3,2,1,0:T(8,128)(2,1)S(1)}, bf16[2,2,64,256]{3,2,1,0:T(8,128)(2,1)S(1)}, u32[]{:S(2)}, u32[]{:S(2)}) collective-permute-start(bf16[2,2,64,256]{3,2,1,0:T(8,128)(2,1)S(1)} %pad_maximum_fusion.1.refs_0_), channel_id=1, source_target_pairs={{0,4},{1,5},{2,6},{3,7},{4,8},{5,9},{6,10},{7,11},{8,12},{9,13},{1... | collective-permute-start | bytes 393224 | tf_op jit(solution)/shard_map/ppermute | solution.py:23
  4.8 2.4 %collective-permute-start.6 = (bf16[2,2,64,256]{3,2,1,0:T(8,128)(2,1)S(1)}, bf16[2,2,64,256]{3,2,1,0:T(8,128)(2,1)S(1)}, u32[]{:S(2)}, u32[]{:S(2)}) collective-permute-start(bf16[2,2,64,256]{3,2,1,0:T(8,128)(2,1)S(1)} %pad_maximum_fusion.2), channel_id=1, source_target_pairs={{0,6},{1,7},{2,4},{3,5},{4,10},{5,11},{6,8},{7,9},{8,14},{9,15},{1... | collective-permute-start | bytes 393224 | tf_op jit(solution)/shard_map/ppermute | solution.py:23
  7.3 1.6 %collective-permute-start.7 = (bf16[2,2,64,256]{3,2,1,0:T(8,128)(2,1)S(1)}, bf16[2,2,64,256]{3,2,1,0:T(8,128)(2,1)S(1)}, u32[]{:S(2)}, u32[]{:S(2)}) collective-permute-start(bf16[2,2,64,256]{3,2,1,0:T(8,128)(2,1)S(1)} %pad_maximum_fusion.1.refs_0_), channel_id=1, source_target_pairs={{0,8},{1,9},{2,10},{3,11},{4,12},{5,13},{6,14},{7,15},{8,16},{9,17... | collective-permute-start | bytes 393224 | tf_op jit(solution)/shard_map/ppermute | solution.py:23
  8.9 1.5 %collective-permute-start.8 = (bf16[2,2,64,256]{3,2,1,0:T(8,128)(2,1)S(1)}, bf16[2,2,64,256]{3,2,1,0:T(8,128)(2,1)S(1)}, u32[]{:S(2)}, u32[]{:S(2)}) collective-permute-start(bf16[2,2,64,256]{3,2,1,0:T(8,128)(2,1)S(1)} %pad_maximum_fusion.2), channel_id=1, source_target_pairs={{0,10},{1,11},{2,8},{3,9},{4,14},{5,15},{6,12},{7,13},{8,18},{9,19... | collective-permute-start | bytes 393224 | tf_op jit(solution)/shard_map/ppermute | solution.py:23
  10.4 0.0 copy-start
  10.4 1.4 %plan.1 = (s32[1]{0:T(128)}, s32[1]{0:T(128)}, s32[3,8,128]{2,1,0:T(8,128)}) custom-call(s32[4]{0:T(128)} %docs_ref.1, s32[1]{0:T(128)} %bitcast.index_ref), custom_call_target="tpu_custom_call" | custom-call | flops 1000000000 | bytes 1048576 | tf_op jit(solution)/shard_map/plan/pallas_call | solution.py:236
  12.4 0.0 collective-permute-done.4.refs_1_
  12.4 0.7 %conditional.1 = (bf16[2,2,64,256]{3,2,1,0:T(8,128)(2,1)}) conditional(s32[]{:T(128)} %bitcast.7, bf16[2,2,64,256]{3,2,1,0:T(8,128)(2,1)S(1)} %pad_maximum_fusion.1.refs_0_, (s32[]{:T(128)}, bf16[2,2,64,256]{3,2,1,0:T(8,128)(2,1)S(1)}, bf16[2,2,64,256]{3,2,1,0:T(8,128)(2,1)S(1)}) %tuple.18, (s32[]{:T(128)}, ...), branch_computations={%region_0.1_spmd, %region_1.2_spmd, %region_2.3_spmd, %region_3.4_... | conditional | flops 65537 | bytes 917562 | solution.py:259
  12.4 0.7 %copy.7 = bf16[2,2,64,256]{3,2,1,0:T(8,128)(2,1)} copy(bf16[2,2,64,256]{3,2,1,0:T(8,128)(2,1)S(1)} %param) | data formatting | bytes 262144 | tf_op jit(solution)/shard_map/cond
  13.1 0.0 copy-done
  13.1 0.0 copy-start.1
  13.1 0.7 %copy-done.1 = s32[3,8,128]{2,1,0:T(8,128)S(1)} copy-done((s32[3,8,128]{2,1,0:T(8,128)S(1)}, s32[3,8,128]{2,1,0:T(8,128)}, u32[]{:S(2)}) %copy-start.1) | copy-done | bytes 12312
  13.8 1.8 %own.1 = (f32[4096,128]{1,0:T(8,128)S(1)}, f32[4096,128]{1,0:T(8,128)S(1)}, f32[4096,128]{1,0:T(8,128)S(1)}) custom-call(s32[3,8,128]{2,1,0:T(8,128)S(1)} %copy-done.1, bf16[256,16,128]{2,1,0:T(8,128)(2,1)S(1)} %copy-done, bf16[2,2,64,256]{3,2,1,0:T(8,128)(2,1)S(1)} %pad_maximum_fusion.1.refs_0_, bf16[2,2,64,256]{3,2,1,0:T(8,128)(2,1)S(1)} %collective-permute-done.4.refs_1_), custom_call_target="tpu_custom_call" | custom-call | flops 100000000 | bytes 1048576 | tf_op jit(solution)/shard_map/own/pallas_call | solution.py:271
  15.5 0.0 collective-permute-done.5.refs_0_
  15.5 0.0 collective-permute-done.6.refs_1_
  15.6 0.7 %one.1 = (f32[4096,128]{1,0:T(8,128)S(1)}, f32[4096,128]{1,0:T(8,128)S(1)}, f32[4096,128]{1,0:T(8,128)S(1)}) custom-call(s32[3,8,128]{2,1,0:T(8,128)S(1)} %copy-done.1, bf16[256,16,128]{2,1,0:T(8,128)(2,1)S(1)} %copy-done, f32[4096,128]{1,0:T(8,128)S(1)} %get-tuple-element.53.summed_in, f32[4096,128]{1,0:T(8,128)S(1)} %get-tuple-element.54.top_in, ...), custom_call_target="tpu_custom_call" | custom-call | flops 100000000 | bytes 1048576 | tf_op jit(solution)/shard_map/one/pallas_call | solution.py:281
  16.3 0.5 %collective-permute-done.7.refs_0_ = bf16[2,2,64,256]{3,2,1,0:T(8,128)(2,1)S(1)} collective-permute-done((bf16[2,2,64,256]{3,2,1,0:T(8,128)(2,1)S(1)}, bf16[2,2,64,256]{3,2,1,0:T(8,128)(2,1)S(1)}, u32[]{:S(2)}, u32[]{:S(2)}) %collective-permute-start.7) | collective-permute-done | bytes 131104 | tf_op jit(solution)/shard_map/ppermute | solution.py:23
  16.7 3.1 %collective-permute-done.8.refs_1_ = bf16[2,2,64,256]{3,2,1,0:T(8,128)(2,1)S(1)} collective-permute-done((bf16[2,2,64,256]{3,2,1,0:T(8,128)(2,1)S(1)}, bf16[2,2,64,256]{3,2,1,0:T(8,128)(2,1)S(1)}, u32[]{:S(2)}, u32[]{:S(2)}) %collective-permute-start.8) | collective-permute-done | bytes 131104 | tf_op jit(solution)/shard_map/ppermute | solution.py:23
  19.8 1.6 %far.1 = bf16[256,16,128]{2,1,0:T(8,128)(2,1)} custom-call(s32[3,8,128]{2,1,0:T(8,128)S(1)} %copy-done.1, bf16[256,16,128]{2,1,0:T(8,128)(2,1)S(1)} %copy-done, f32[4096,128]{1,0:T(8,128)S(1)} %get-tuple-element.56.summed_in, f32[4096,128]{1,0:T(8,128)S(1)} %get-tuple-element.57.top_in, f32[4096,128]{1,0:T(8,128)S(1)} %get-tuple-element.58.total_in, ...), custom_call_target="tpu_custom_call" | custom-call | flops 100000000 | bytes 1048576 | tf_op jit(solution)/shard_map/far/pallas_call | solution.py:291
  (6 shorter events, 0.1 us)
Async XLA Ops:
  1.2 1.4 %collective-permute-start.3 = (bf16[2,2,64,256]{3,2,1,0:T(8,128)(2,1)S(1)}, bf16[2,2,64,256]{3,2,1,0:T(8,128)(2,1)S(1)}, u32[]{:S(2)}, u32[]{:S(2)}) collective-permute-start(bf16[2,2,64,256]{3,2,1,0:T(8,128)(2,1)S(1)} %slice_bitcast_fusion), channel_id=1, source_target_pairs={{0,1},{1,0},{2,3},{3,2},{4,5},{5,4},{6,7},{7,6},{8,9},{9,8},{10,11... | collective-permute-start | bytes 393224 | tf_op jit(solution)/shard_map/ppermute | solution.py:23
  2.6 9.7 %collective-permute-start.4 = (bf16[2,2,64,256]{3,2,1,0:T(8,128)(2,1)S(1)}, bf16[2,2,64,256]{3,2,1,0:T(8,128)(2,1)S(1)}, u32[]{:S(2)}, u32[]{:S(2)}) collective-permute-start(bf16[2,2,64,256]{3,2,1,0:T(8,128)(2,1)S(1)} %pad_maximum_fusion.2), channel_id=1, source_target_pairs={{0,2},{1,3},{2,0},{3,1},{4,6},{5,7},{6,4},{7,5},{8,10},{9,11},{10,... | collective-permute-start | bytes 393224 | tf_op jit(solution)/shard_map/ppermute | solution.py:23
  3.2 12.3 %collective-permute-start.5 = (bf16[2,2,64,256]{3,2,1,0:T(8,128)(2,1)S(1)}, bf16[2,2,64,256]{3,2,1,0:T(8,128)(2,1)S(1)}, u32[]{:S(2)}, u32[]{:S(2)}) collective-permute-start(bf16[2,2,64,256]{3,2,1,0:T(8,128)(2,1)S(1)} %pad_maximum_fusion.1.refs_0_), channel_id=1, source_target_pairs={{0,4},{1,5},{2,6},{3,7},{4,8},{5,9},{6,10},{7,11},{8,12},{9,13},{1... | collective-permute-start | bytes 393224 | tf_op jit(solution)/shard_map/ppermute | solution.py:23
  4.8 10.7 %collective-permute-start.6 = (bf16[2,2,64,256]{3,2,1,0:T(8,128)(2,1)S(1)}, bf16[2,2,64,256]{3,2,1,0:T(8,128)(2,1)S(1)}, u32[]{:S(2)}, u32[]{:S(2)}) collective-permute-start(bf16[2,2,64,256]{3,2,1,0:T(8,128)(2,1)S(1)} %pad_maximum_fusion.2), channel_id=1, source_target_pairs={{0,6},{1,7},{2,4},{3,5},{4,10},{5,11},{6,8},{7,9},{8,14},{9,15},{1... | collective-permute-start | bytes 393224 | tf_op jit(solution)/shard_map/ppermute | solution.py:23
  7.3 9.4 %collective-permute-start.7 = (bf16[2,2,64,256]{3,2,1,0:T(8,128)(2,1)S(1)}, bf16[2,2,64,256]{3,2,1,0:T(8,128)(2,1)S(1)}, u32[]{:S(2)}, u32[]{:S(2)}) collective-permute-start(bf16[2,2,64,256]{3,2,1,0:T(8,128)(2,1)S(1)} %pad_maximum_fusion.1.refs_0_), channel_id=1, source_target_pairs={{0,8},{1,9},{2,10},{3,11},{4,12},{5,13},{6,14},{7,15},{8,16},{9,17... | collective-permute-start | bytes 393224 | tf_op jit(solution)/shard_map/ppermute | solution.py:23
  8.9 10.9 %collective-permute-start.8 = (bf16[2,2,64,256]{3,2,1,0:T(8,128)(2,1)S(1)}, bf16[2,2,64,256]{3,2,1,0:T(8,128)(2,1)S(1)}, u32[]{:S(2)}, u32[]{:S(2)}) collective-permute-start(bf16[2,2,64,256]{3,2,1,0:T(8,128)(2,1)S(1)} %pad_maximum_fusion.2), channel_id=1, source_target_pairs={{0,10},{1,11},{2,8},{3,9},{4,14},{5,15},{6,12},{7,13},{8,18},{9,19... | collective-permute-start | bytes 393224 | tf_op jit(solution)/shard_map/ppermute | solution.py:23
  10.4 2.7 %copy-start = (bf16[256,16,128]{2,1,0:T(8,128)(2,1)S(1)}, bf16[256,16,128]{2,1,0:T(8,128)(2,1)}, u32[]{:S(2)}) copy-start(bf16[256,16,128]{2,1,0:T(8,128)(2,1)} %query_ref.5) | copy-start | bytes 3145732
  13.1 0.7 %copy-start.1 = (s32[3,8,128]{2,1,0:T(8,128)S(1)}, s32[3,8,128]{2,1,0:T(8,128)}, u32[]{:S(2)}) copy-start(s32[3,8,128]{2,1,0:T(8,128)} %get-tuple-element.49.behind_ref) | copy-start | bytes 36868

commit v4 on v3

--- a/solution.py
+++ b/solution.py
@@ -228,7 +228,7 @@
     params = pltpu.CompilerParams(vmem_limit_bytes=24 * 1024 * 1024)
     scale = 1.0 / math.sqrt(depth)
     light, medium = (
-        pl.CostEstimate(flops=flops, bytes_accessed=2**20, transcendentals=10**6) for flops in (10**8, 10**9)
+        pl.CostEstimate(flops=flops, bytes_accessed=2**20, transcendentals=10**6) for flops in (10**9, 10**9)
     )
     shape = jax.ShapeDtypeStruct
     me = lax.axis_index("kvh")

time: 21.9 us -> 23 us (1.050)
  the two profiles are of different devices: /device:TPU:6 before, /device:TPU:0 now
where the time goes in v4:
time: 23 us; the launch traced here: 22.8 us
  starting transfers between devices  10.6 us (46%)
  Pallas kernels  5.5 us (24%)
  waiting for transfers between devices  3.26 us (14%)
  local copies, waits for them, and re-layouts  1.44 us (6%)
  other arithmetic  1.13 us (5%)
  between operations  0.81 us (4%)
    ppermute x6, starting transfers between devices, passed_along(): return lax.ppermute(piece, ('ctx', 'kvh'), pairs)  10.6 us
    ppermute x6, waiting for transfers between devices, passed_along(): return lax.ppermute(piece, ('ctx', 'kvh'), pairs)  3.26 us
    pallas_call x1, Pallas kernels, body(): pl.pallas_call(functools.partial(own_kernel, scale), out_shape=state, in_...  1.75 us
    pallas_call x1, Pallas kernels, body(): pl.pallas_call(functools.partial(join_kernel, scale, per_shard, True), ou...  1.58 us
    pallas_call x1, Pallas kernels, body(): pl.pallas_call(functools.partial(plan_kernel, parts, behind), cost_estima...  1.44 us
    concatenate x1, other arithmetic, body(): both = lax.optimization_barrier(jnp.concatenate([keys, values], axis=2))  1 us
    pallas_call x1, Pallas kernels, body(): pl.pallas_call(functools.partial(join_kernel, scale, 0, False), out_shape...  0.72 us
    unnamed x4, local copies, waits for them, and re-layouts  0.71 us
  transfers between devices with their start and end apart: 6, of which 2 were waited for; matrix products, arithmetic and copies ran while one was open for 3% of the time, Pallas kernels for 17%

profile of v4, /device:TPU:0, one launch (start us, length us, event | category | flops | bytes accessed | tf_op | source)
XLA Modules:
  0.0 22.8 jit_solution(6554343842608934651)
XLA Ops:
  0.0 1.0 %pad_maximum_fusion = bf16[64,8,256]{2,1,0:T(8,128)(2,1)S(1)} fusion(bf16[64,8,128]{2,1,0:T(8,128)(2,1)} %param.10, bf16[64,8,128]{2,1,0:T(8,128)(2,1)} %param.9), kind=kLoop, calls=%fused_computation.5 | loop fusion | flops 524288 | bytes 524288 | tf_op jit(solution)/shard_map/concatenate | solution.py:244
  1.1 0.1 reverse_select_fusion.1
  1.1 0.1 reverse_select_fusion
  1.2 0.5 %collective-permute-start.3 = (bf16[2,2,64,256]{3,2,1,0:T(8,128)(2,1)S(1)}, bf16[2,2,64,256]{3,2,1,0:T(8,128)(2,1)S(1)}, u32[]{:S(2)}, u32[]{:S(2)}) collective-permute-start(bf16[2,2,64,256]{3,2,1,0:T(8,128)(2,1)S(1)} %slice_bitcast_fusion), channel_id=1, source_target_pairs={{0,1},{1,0},{2,3},{3,2},{4,5},{5,4},{6,7},{7,6},{8,9},{9,8},{10,11... | collective-permute-start | bytes 393224 | tf_op jit(solution)/shard_map/ppermute | solution.py:23
  1.7 1.0 %collective-permute-done.3 = bf16[2,2,64,256]{3,2,1,0:T(8,128)(2,1)S(1)} collective-permute-done((bf16[2,2,64,256]{3,2,1,0:T(8,128)(2,1)S(1)}, bf16[2,2,64,256]{3,2,1,0:T(8,128)(2,1)S(1)}, u32[]{:S(2)}, u32[]{:S(2)}) %collective-permute-start.3) | collective-permute-done | bytes 131104 | tf_op jit(solution)/shard_map/ppermute | solution.py:23
  2.7 3.9 %collective-permute-start.6 = (bf16[2,2,64,256]{3,2,1,0:T(8,128)(2,1)S(1)}, bf16[2,2,64,256]{3,2,1,0:T(8,128)(2,1)S(1)}, u32[]{:S(2)}, u32[]{:S(2)}) collective-permute-start(bf16[2,2,64,256]{3,2,1,0:T(8,128)(2,1)S(1)} %pad_maximum_fusion.2), channel_id=1, source_target_pairs={{0,6},{1,7},{2,4},{3,5},{4,10},{5,11},{6,8},{7,9},{8,14},{9,15},{1... | collective-permute-start | bytes 393224 | tf_op jit(solution)/shard_map/ppermute | solution.py:23
  6.6 0.5 %collective-permute-start.4 = (bf16[2,2,64,256]{3,2,1,0:T(8,128)(2,1)S(1)}, bf16[2,2,64,256]{3,2,1,0:T(8,128)(2,1)S(1)}, u32[]{:S(2)}, u32[]{:S(2)}) collective-permute-start(bf16[2,2,64,256]{3,2,1,0:T(8,128)(2,1)S(1)} %pad_maximum_fusion.2), channel_id=1, source_target_pairs={{0,2},{1,3},{2,0},{3,1},{4,6},{5,7},{6,4},{7,5},{8,10},{9,11},{10,... | collective-permute-start | bytes 393224 | tf_op jit(solution)/shard_map/ppermute | solution.py:23
  7.1 1.6 %collective-permute-start.5 = (bf16[2,2,64,256]{3,2,1,0:T(8,128)(2,1)S(1)}, bf16[2,2,64,256]{3,2,1,0:T(8,128)(2,1)S(1)}, u32[]{:S(2)}, u32[]{:S(2)}) collective-permute-start(bf16[2,2,64,256]{3,2,1,0:T(8,128)(2,1)S(1)} %pad_maximum_fusion.1.refs_0_), channel_id=1, source_target_pairs={{0,4},{1,5},{2,6},{3,7},{4,8},{5,9},{6,10},{7,11},{8,12},{9,13},{1... | collective-permute-start | bytes 393224 | tf_op jit(solution)/shard_map/ppermute | solution.py:23
  8.7 0.0 copy-start
  8.7 1.4 %plan.1 = (s32[1]{0:T(128)}, s32[1]{0:T(128)}, s32[3,8,128]{2,1,0:T(8,128)}) custom-call(s32[4]{0:T(128)} %docs_ref.1, s32[1]{0:T(128)} %bitcast.index_ref), custom_call_target="tpu_custom_call" | custom-call | flops 1000000000 | bytes 1048576 | tf_op jit(solution)/shard_map/plan/pallas_call | solution.py:236
  10.7 1.6 %collective-permute-start.7 = (bf16[2,2,64,256]{3,2,1,0:T(8,128)(2,1)S(1)}, bf16[2,2,64,256]{3,2,1,0:T(8,128)(2,1)S(1)}, u32[]{:S(2)}, u32[]{:S(2)}) collective-permute-start(bf16[2,2,64,256]{3,2,1,0:T(8,128)(2,1)S(1)} %pad_maximum_fusion.1.refs_0_), channel_id=1, source_target_pairs={{0,8},{1,9},{2,10},{3,11},{4,12},{5,13},{6,14},{7,15},{8,16},{9,17... | collective-permute-start | bytes 393224 | tf_op jit(solution)/shard_map/ppermute | solution.py:23
  12.3 2.5 %collective-permute-start.8 = (bf16[2,2,64,256]{3,2,1,0:T(8,128)(2,1)S(1)}, bf16[2,2,64,256]{3,2,1,0:T(8,128)(2,1)S(1)}, u32[]{:S(2)}, u32[]{:S(2)}) collective-permute-start(bf16[2,2,64,256]{3,2,1,0:T(8,128)(2,1)S(1)} %pad_maximum_fusion.2), channel_id=1, source_target_pairs={{0,10},{1,11},{2,8},{3,9},{4,14},{5,15},{6,12},{7,13},{8,18},{9,19... | collective-permute-start | bytes 393224 | tf_op jit(solution)/shard_map/ppermute | solution.py:23
  14.9 0.0 collective-permute-done.4.refs_1_
  14.9 0.7 %conditional.1 = (bf16[2,2,64,256]{3,2,1,0:T(8,128)(2,1)}) conditional(s32[]{:T(128)} %bitcast.7, bf16[2,2,64,256]{3,2,1,0:T(8,128)(2,1)S(1)} %pad_maximum_fusion.1.refs_0_, (s32[]{:T(128)}, bf16[2,2,64,256]{3,2,1,0:T(8,128)(2,1)S(1)}, bf16[2,2,64,256]{3,2,1,0:T(8,128)(2,1)S(1)}) %tuple.18, (s32[]{:T(128)}, ...), branch_computations={%region_0.1_spmd, %region_1.2_spmd, %region_2.3_spmd, %region_3.4_... | conditional | flops 65537 | bytes 917562 | solution.py:259
  14.9 0.7 %copy.7 = bf16[2,2,64,256]{3,2,1,0:T(8,128)(2,1)} copy(bf16[2,2,64,256]{3,2,1,0:T(8,128)(2,1)S(1)} %param) | data formatting | bytes 262144 | tf_op jit(solution)/shard_map/cond
  15.5 0.0 copy-done
  15.5 0.0 copy-start.1
  15.5 0.7 %copy-done.1 = s32[3,8,128]{2,1,0:T(8,128)S(1)} copy-done((s32[3,8,128]{2,1,0:T(8,128)S(1)}, s32[3,8,128]{2,1,0:T(8,128)}, u32[]{:S(2)}) %copy-start.1) | copy-done | bytes 12312
  16.2 1.8 %own.1 = (f32[4096,128]{1,0:T(8,128)S(1)}, f32[4096,128]{1,0:T(8,128)S(1)}, f32[4096,128]{1,0:T(8,128)S(1)}) custom-call(s32[3,8,128]{2,1,0:T(8,128)S(1)} %copy-done.1, bf16[256,16,128]{2,1,0:T(8,128)(2,1)S(1)} %copy-done, bf16[2,2,64,256]{3,2,1,0:T(8,128)(2,1)S(1)} %pad_maximum_fusion.1.refs_0_, bf16[2,2,64,256]{3,2,1,0:T(8,128)(2,1)S(1)} %collective-permute-done.4.refs_1_), custom_call_target="tpu_custom_call" | custom-call | flops 1000000000 | bytes 1048576 | tf_op jit(solution)/shard_map/own/pallas_call | solution.py:271
  18.0 0.0 collective-permute-done.5.refs_0_
  18.0 0.0 collective-permute-done.6.refs_1_
  18.0 0.7 %one.1 = (f32[4096,128]{1,0:T(8,128)S(1)}, f32[4096,128]{1,0:T(8,128)S(1)}, f32[4096,128]{1,0:T(8,128)S(1)}) custom-call(s32[3,8,128]{2,1,0:T(8,128)S(1)} %copy-done.1, bf16[256,16,128]{2,1,0:T(8,128)(2,1)S(1)} %copy-done, f32[4096,128]{1,0:T(8,128)S(1)} %get-tuple-element.53.summed_in, f32[4096,128]{1,0:T(8,128)S(1)} %get-tuple-element.54.top_in, ...), custom_call_target="tpu_custom_call" | custom-call | flops 1000000000 | bytes 1048576 | tf_op jit(solution)/shard_map/one/pallas_call | solution.py:281
  18.8 0.0 collective-permute-done.7.refs_0_
  18.8 2.3 %collective-permute-done.8.refs_1_ = bf16[2,2,64,256]{3,2,1,0:T(8,128)(2,1)S(1)} collective-permute-done((bf16[2,2,64,256]{3,2,1,0:T(8,128)(2,1)S(1)}, bf16[2,2,64,256]{3,2,1,0:T(8,128)(2,1)S(1)}, u32[]{:S(2)}, u32[]{:S(2)}) %collective-permute-start.8) | collective-permute-done | bytes 131104 | tf_op jit(solution)/shard_map/ppermute | solution.py:23
  21.0 1.6 %far.1 = bf16[256,16,128]{2,1,0:T(8,128)(2,1)} custom-call(s32[3,8,128]{2,1,0:T(8,128)S(1)} %copy-done.1, bf16[256,16,128]{2,1,0:T(8,128)(2,1)S(1)} %copy-done, f32[4096,128]{1,0:T(8,128)S(1)} %get-tuple-element.56.summed_in, f32[4096,128]{1,0:T(8,128)S(1)} %get-tuple-element.57.top_in, f32[4096,128]{1,0:T(8,128)S(1)} %get-tuple-element.58.total_in, ...), custom_call_target="tpu_custom_call" | custom-call | flops 1000000000 | bytes 1048576 | tf_op jit(solution)/shard_map/far/pallas_call | solution.py:291
  (6 shorter events, 0.1 us)
Async XLA Ops:
  1.2 1.5 %collective-permute-start.3 = (bf16[2,2,64,256]{3,2,1,0:T(8,128)(2,1)S(1)}, bf16[2,2,64,256]{3,2,1,0:T(8,128)(2,1)S(1)}, u32[]{:S(2)}, u32[]{:S(2)}) collective-permute-start(bf16[2,2,64,256]{3,2,1,0:T(8,128)(2,1)S(1)} %slice_bitcast_fusion), channel_id=1, source_target_pairs={{0,1},{1,0},{2,3},{3,2},{4,5},{5,4},{6,7},{7,6},{8,9},{9,8},{10,11... | collective-permute-start | bytes 393224 | tf_op jit(solution)/shard_map/ppermute | solution.py:23
  2.7 15.3 %collective-permute-start.6 = (bf16[2,2,64,256]{3,2,1,0:T(8,128)(2,1)S(1)}, bf16[2,2,64,256]{3,2,1,0:T(8,128)(2,1)S(1)}, u32[]{:S(2)}, u32[]{:S(2)}) collective-permute-start(bf16[2,2,64,256]{3,2,1,0:T(8,128)(2,1)S(1)} %pad_maximum_fusion.2), channel_id=1, source_target_pairs={{0,6},{1,7},{2,4},{3,5},{4,10},{5,11},{6,8},{7,9},{8,14},{9,15},{1... | collective-permute-start | bytes 393224 | tf_op jit(solution)/shard_map/ppermute | solution.py:23
  6.6 8.3 %collective-permute-start.4 = (bf16[2,2,64,256]{3,2,1,0:T(8,128)(2,1)S(1)}, bf16[2,2,64,256]{3,2,1,0:T(8,128)(2,1)S(1)}, u32[]{:S(2)}, u32[]{:S(2)}) collective-permute-start(bf16[2,2,64,256]{3,2,1,0:T(8,128)(2,1)S(1)} %pad_maximum_fusion.2), channel_id=1, source_target_pairs={{0,2},{1,3},{2,0},{3,1},{4,6},{5,7},{6,4},{7,5},{8,10},{9,11},{10,... | collective-permute-start | bytes 393224 | tf_op jit(solution)/shard_map/ppermute | solution.py:23
  7.1 10.9 %collective-permute-start.5 = (bf16[2,2,64,256]{3,2,1,0:T(8,128)(2,1)S(1)}, bf16[2,2,64,256]{3,2,1,0:T(8,128)(2,1)S(1)}, u32[]{:S(2)}, u32[]{:S(2)}) collective-permute-start(bf16[2,2,64,256]{3,2,1,0:T(8,128)(2,1)S(1)} %pad_maximum_fusion.1.refs_0_), channel_id=1, source_target_pairs={{0,4},{1,5},{2,6},{3,7},{4,8},{5,9},{6,10},{7,11},{8,12},{9,13},{1... | collective-permute-start | bytes 393224 | tf_op jit(solution)/shard_map/ppermute | solution.py:23
  8.7 6.8 %copy-start = (bf16[256,16,128]{2,1,0:T(8,128)(2,1)S(1)}, bf16[256,16,128]{2,1,0:T(8,128)(2,1)}, u32[]{:S(2)}) copy-start(bf16[256,16,128]{2,1,0:T(8,128)(2,1)} %query_ref.5) | copy-start | bytes 3145732
  10.7 8.0 %collective-permute-start.7 = (bf16[2,2,64,256]{3,2,1,0:T(8,128)(2,1)S(1)}, bf16[2,2,64,256]{3,2,1,0:T(8,128)(2,1)S(1)}, u32[]{:S(2)}, u32[]{:S(2)}) collective-permute-start(bf16[2,2,64,256]{3,2,1,0:T(8,128)(2,1)S(1)} %pad_maximum_fusion.1.refs_0_), channel_id=1, source_target_pairs={{0,8},{1,9},{2,10},{3,11},{4,12},{5,13},{6,14},{7,15},{8,16},{9,17... | collective-permute-start | bytes 393224 | tf_op jit(solution)/shard_map/ppermute | solution.py:23
  12.3 8.7 %collective-permute-start.8 = (bf16[2,2,64,256]{3,2,1,0:T(8,128)(2,1)S(1)}, bf16[2,2,64,256]{3,2,1,0:T(8,128)(2,1)S(1)}, u32[]{:S(2)}, u32[]{:S(2)}) collective-permute-start(bf16[2,2,64,256]{3,2,1,0:T(8,128)(2,1)S(1)} %pad_maximum_fusion.2), channel_id=1, source_target_pairs={{0,10},{1,11},{2,8},{3,9},{4,14},{5,15},{6,12},{7,13},{8,18},{9,19... | collective-permute-start | bytes 393224 | tf_op jit(solution)/shard_map/ppermute | solution.py:23
  15.5 0.7 %copy-start.1 = (s32[3,8,128]{2,1,0:T(8,128)S(1)}, s32[3,8,128]{2,1,0:T(8,128)}, u32[]{:S(2)}) copy-start(s32[3,8,128]{2,1,0:T(8,128)} %get-tuple-element.49.behind_ref) | copy-start | bytes 36868

commit v5 on v3

--- a/solution.py
+++ b/solution.py
@@ -245,6 +245,7 @@
     both = both.reshape(tokens, parts, count, 2 * depth).transpose(1, 2, 0, 3)
     pieces = for_groups(both, me)
     swapped = passed_along(pieces[:, 1], 0, across=1)
+    swapped, spans, last, nearer = lax.optimization_barrier((swapped, spans, last, nearer))
     here, there = (jnp.stack([pieces[side, 0], swapped[side]]) for side in range(2))
     own = [here, passed_along(there, 0, across=2)]
     far = [passed_along(here, 2), passed_along(there, 2, across=2)]

time: 21.9 us -> 22.4 us (1.023)
  Pallas kernels: 5.5 us -> 7.23 us
  local copies, waits for them, and re-layouts: 1.45 us -> 0.75 us
  waiting for transfers between devices: 4.85 us -> 4.3 us
    pallas_call x1, Pallas kernels: 0.72 us -> 2.45 us  [body(): pl.pallas_call(functools.partial(join_kernel, scale, 0, False), out_shape...]
    unnamed x4, local copies, waits for them, and re-layouts: 0.71 us -> 0.01 us
    ppermute x6, waiting for transfers between devices: 4.85 us -> 4.3 us  [passed_along(): return lax.ppermute(piece, ('ctx', 'kvh'), pairs)]
  transfers between devices with their start and end apart: 6 -> 6, of which waited for: 3 -> 2; matrix products, arithmetic and copies ran while one was open for 3% -> 3% of each run, Pallas kernels for 18% -> 26%
where the time goes in v5:
time: 22.4 us; the launch traced here: 22.1 us
  starting transfers between devices  7.79 us (35%)
  Pallas kernels  7.23 us (32%)
  waiting for transfers between devices  4.3 us (19%)
  other arithmetic  1.13 us (5%)
  between operations  0.86 us (4%)
  local copies, waits for them, and re-layouts  0.75 us (3%)
    ppermute x6, starting transfers between devices, passed_along(): return lax.ppermute(piece, ('ctx', 'kvh'), pairs)  7.79 us
    ppermute x6, waiting for transfers between devices, passed_along(): return lax.ppermute(piece, ('ctx', 'kvh'), pairs)  4.3 us
    pallas_call x1, Pallas kernels, body(): pl.pallas_call(functools.partial(join_kernel, scale, 0, False), out_shape...  2.45 us
    pallas_call x1, Pallas kernels, body(): pl.pallas_call(functools.partial(own_kernel, scale), out_shape=state, in_...  1.75 us
    pallas_call x1, Pallas kernels, body(): pl.pallas_call(functools.partial(join_kernel, scale, per_shard, True), ou...  1.58 us
    pallas_call x1, Pallas kernels, body(): pl.pallas_call(functools.partial(plan_kernel, parts, behind), cost_estima...  1.45 us
    concatenate x1, other arithmetic, body(): both = lax.optimization_barrier(jnp.concatenate([keys, values], axis=2))  1 us
    cond x1, local copies, waits for them, and re-layouts  0.65 us
  transfers between devices with their start and end apart: 6, of which 2 were waited for; matrix products, arithmetic and copies ran while one was open for 3% of the time, Pallas kernels for 26%

profile of v5, /device:TPU:6, one launch (start us, length us, event | category | flops | bytes accessed | tf_op | source)
XLA Modules:
  0.0 22.1 jit_solution(6896592287702255707)
XLA Ops:
  0.0 1.0 %pad_maximum_fusion = bf16[64,8,256]{2,1,0:T(8,128)(2,1)S(1)} fusion(bf16[64,8,128]{2,1,0:T(8,128)(2,1)} %param.10, bf16[64,8,128]{2,1,0:T(8,128)(2,1)} %param.9), kind=kLoop, calls=%fused_computation.5 | loop fusion | flops 524288 | bytes 524288 | tf_op jit(solution)/shard_map/concatenate | solution.py:244
  1.1 0.1 reverse_select_fusion.1
  1.1 0.1 reverse_select_fusion
  1.2 0.1 collective-permute-start.3
  1.3 0.0 copy-start
  1.3 1.4 %plan.1 = (s32[1]{0:T(128)}, s32[1]{0:T(128)}, s32[3,8,128]{2,1,0:T(8,128)}) custom-call(s32[4]{0:T(128)} %docs_ref.1, s32[1]{0:T(128)} %bitcast.4.index_ref), custom_call_target="tpu_custom_call" | custom-call | flops 1000000000 | bytes 1048576 | tf_op jit(solution)/shard_map/plan/pallas_call | solution.py:236
  2.8 0.0 copy-start.1
  2.8 0.0 collective-permute-done.3
  2.8 0.6 %collective-permute-start.4 = (bf16[2,2,64,256]{3,2,1,0:T(8,128)(2,1)S(1)}, bf16[2,2,64,256]{3,2,1,0:T(8,128)(2,1)S(1)}, u32[]{:S(2)}, u32[]{:S(2)}) collective-permute-start(bf16[2,2,64,256]{3,2,1,0:T(8,128)(2,1)S(1)} %pad_maximum_fusion.2), channel_id=1, source_target_pairs={{0,2},{1,3},{2,0},{3,1},{4,6},{5,7},{6,4},{7,5},{8,10},{9,11},{10,... | collective-permute-start | bytes 393224 | tf_op jit(solution)/shard_map/ppermute | solution.py:23
  3.4 1.6 %collective-permute-start.5 = (bf16[2,2,64,256]{3,2,1,0:T(8,128)(2,1)S(1)}, bf16[2,2,64,256]{3,2,1,0:T(8,128)(2,1)S(1)}, u32[]{:S(2)}, u32[]{:S(2)}) collective-permute-start(bf16[2,2,64,256]{3,2,1,0:T(8,128)(2,1)S(1)} %pad_maximum_fusion.1.refs_0_), channel_id=1, source_target_pairs={{0,4},{1,5},{2,6},{3,7},{4,8},{5,9},{6,10},{7,11},{8,12},{9,13},{1... | collective-permute-start | bytes 393224 | tf_op jit(solution)/shard_map/ppermute | solution.py:23
  5.0 2.4 %collective-permute-start.6 = (bf16[2,2,64,256]{3,2,1,0:T(8,128)(2,1)S(1)}, bf16[2,2,64,256]{3,2,1,0:T(8,128)(2,1)S(1)}, u32[]{:S(2)}, u32[]{:S(2)}) collective-permute-start(bf16[2,2,64,256]{3,2,1,0:T(8,128)(2,1)S(1)} %pad_maximum_fusion.2), channel_id=1, source_target_pairs={{0,6},{1,7},{2,4},{3,5},{4,10},{5,11},{6,8},{7,9},{8,14},{9,15},{1... | collective-permute-start | bytes 393224 | tf_op jit(solution)/shard_map/ppermute | solution.py:23
  7.5 1.6 %collective-permute-start.7 = (bf16[2,2,64,256]{3,2,1,0:T(8,128)(2,1)S(1)}, bf16[2,2,64,256]{3,2,1,0:T(8,128)(2,1)S(1)}, u32[]{:S(2)}, u32[]{:S(2)}) collective-permute-start(bf16[2,2,64,256]{3,2,1,0:T(8,128)(2,1)S(1)} %pad_maximum_fusion.1.refs_0_), channel_id=1, source_target_pairs={{0,8},{1,9},{2,10},{3,11},{4,12},{5,13},{6,14},{7,15},{8,16},{9,17... | collective-permute-start | bytes 393224 | tf_op jit(solution)/shard_map/ppermute | solution.py:23
  9.0 1.5 %collective-permute-start.8 = (bf16[2,2,64,256]{3,2,1,0:T(8,128)(2,1)S(1)}, bf16[2,2,64,256]{3,2,1,0:T(8,128)(2,1)S(1)}, u32[]{:S(2)}, u32[]{:S(2)}) collective-permute-start(bf16[2,2,64,256]{3,2,1,0:T(8,128)(2,1)S(1)} %pad_maximum_fusion.2), channel_id=1, source_target_pairs={{0,10},{1,11},{2,8},{3,9},{4,14},{5,15},{6,12},{7,13},{8,18},{9,19... | collective-permute-start | bytes 393224 | tf_op jit(solution)/shard_map/ppermute | solution.py:23
  11.1 0.0 collective-permute-done.4.refs_1_
  11.1 0.7 %conditional.1 = (bf16[2,2,64,256]{3,2,1,0:T(8,128)(2,1)}) conditional(s32[]{:T(128)} %bitcast.7, bf16[2,2,64,256]{3,2,1,0:T(8,128)(2,1)S(1)} %pad_maximum_fusion.1.refs_0_, (s32[]{:T(128)}, bf16[2,2,64,256]{3,2,1,0:T(8,128)(2,1)S(1)}, bf16[2,2,64,256]{3,2,1,0:T(8,128)(2,1)S(1)}) %tuple.21, (s32[]{:T(128)}, ...), branch_computations={%region_0.1_spmd, %region_1.2_spmd, %region_2.3_spmd, %region_3.4_... | conditional | flops 65537 | bytes 917562 | solution.py:260
  11.1 0.7 %copy.7 = bf16[2,2,64,256]{3,2,1,0:T(8,128)(2,1)} copy(bf16[2,2,64,256]{3,2,1,0:T(8,128)(2,1)S(1)} %param) | data formatting | bytes 262144 | tf_op jit(solution)/shard_map/cond
  11.8 0.0 copy-done
  11.8 0.0 copy-done.1
  11.8 1.8 %own.1 = (f32[4096,128]{1,0:T(8,128)S(1)}, f32[4096,128]{1,0:T(8,128)S(1)}, f32[4096,128]{1,0:T(8,128)S(1)}) custom-call(s32[3,8,128]{2,1,0:T(8,128)S(1)} %copy-done.1, bf16[256,16,128]{2,1,0:T(8,128)(2,1)S(1)} %copy-done, bf16[2,2,64,256]{3,2,1,0:T(8,128)(2,1)S(1)} %pad_maximum_fusion.1.refs_0_, bf16[2,2,64,256]{3,2,1,0:T(8,128)(2,1)S(1)} %collective-permute-done.4.refs_1_), custom_call_target="tpu_custom_call" | custom-call | flops 100000000 | bytes 1048576 | tf_op jit(solution)/shard_map/own/pallas_call | solution.py:272
  13.6 0.0 collective-permute-done.5.refs_0_
  13.6 0.0 collective-permute-done.6.refs_1_
  13.6 2.4 %one.1 = (f32[4096,128]{1,0:T(8,128)S(1)}, f32[4096,128]{1,0:T(8,128)S(1)}, f32[4096,128]{1,0:T(8,128)S(1)}) custom-call(s32[3,8,128]{2,1,0:T(8,128)S(1)} %copy-done.1, bf16[256,16,128]{2,1,0:T(8,128)(2,1)S(1)} %copy-done, f32[4096,128]{1,0:T(8,128)S(1)} %get-tuple-element.59.summed_in, f32[4096,128]{1,0:T(8,128)S(1)} %get-tuple-element.60.top_in, ...), custom_call_target="tpu_custom_call" | custom-call | flops 100000000 | bytes 1048576 | tf_op jit(solution)/shard_map/one/pallas_call | solution.py:282
  16.0 0.9 %collective-permute-done.7.refs_0_ = bf16[2,2,64,256]{3,2,1,0:T(8,128)(2,1)S(1)} collective-permute-done((bf16[2,2,64,256]{3,2,1,0:T(8,128)(2,1)S(1)}, bf16[2,2,64,256]{3,2,1,0:T(8,128)(2,1)S(1)}, u32[]{:S(2)}, u32[]{:S(2)}) %collective-permute-start.7) | collective-permute-done | bytes 131104 | tf_op jit(solution)/shard_map/ppermute | solution.py:23
  17.0 3.4 %collective-permute-done.8.refs_1_ = bf16[2,2,64,256]{3,2,1,0:T(8,128)(2,1)S(1)} collective-permute-done((bf16[2,2,64,256]{3,2,1,0:T(8,128)(2,1)S(1)}, bf16[2,2,64,256]{3,2,1,0:T(8,128)(2,1)S(1)}, u32[]{:S(2)}, u32[]{:S(2)}) %collective-permute-start.8) | collective-permute-done | bytes 131104 | tf_op jit(solution)/shard_map/ppermute | solution.py:23
  20.3 1.6 %far.1 = bf16[256,16,128]{2,1,0:T(8,128)(2,1)} custom-call(s32[3,8,128]{2,1,0:T(8,128)S(1)} %copy-done.1, bf16[256,16,128]{2,1,0:T(8,128)(2,1)S(1)} %copy-done, f32[4096,128]{1,0:T(8,128)S(1)} %get-tuple-element.62.summed_in, f32[4096,128]{1,0:T(8,128)S(1)} %get-tuple-element.63.top_in, f32[4096,128]{1,0:T(8,128)S(1)} %get-tuple-element.64.total_in, ...), custom_call_target="tpu_custom_call" | custom-call | flops 100000000 | bytes 1048576 | tf_op jit(solution)/shard_map/far/pallas_call | solution.py:292
  (6 shorter events, 0.1 us)
Async XLA Ops:
  1.2 1.6 %collective-permute-start.3 = (bf16[2,2,64,256]{3,2,1,0:T(8,128)(2,1)S(1)}, bf16[2,2,64,256]{3,2,1,0:T(8,128)(2,1)S(1)}, u32[]{:S(2)}, u32[]{:S(2)}) collective-permute-start(bf16[2,2,64,256]{3,2,1,0:T(8,128)(2,1)S(1)} %slice_bitcast_fusion), channel_id=1, source_target_pairs={{0,1},{1,0},{2,3},{3,2},{4,5},{5,4},{6,7},{7,6},{8,9},{9,8},{10,11... | collective-permute-start | bytes 393224 | tf_op jit(solution)/shard_map/ppermute | solution.py:23
  1.3 10.5 %copy-start = (bf16[256,16,128]{2,1,0:T(8,128)(2,1)S(1)}, bf16[256,16,128]{2,1,0:T(8,128)(2,1)}, u32[]{:S(2)}) copy-start(bf16[256,16,128]{2,1,0:T(8,128)(2,1)} %query_ref.5) | copy-start | bytes 3145732
  2.8 9.0 %copy-start.1 = (s32[3,8,128]{2,1,0:T(8,128)S(1)}, s32[3,8,128]{2,1,0:T(8,128)}, u32[]{:S(2)}) copy-start(s32[3,8,128]{2,1,0:T(8,128)} %get-tuple-element.54.behind_ref) | copy-start | bytes 36868
  2.8 8.3 %collective-permute-start.4 = (bf16[2,2,64,256]{3,2,1,0:T(8,128)(2,1)S(1)}, bf16[2,2,64,256]{3,2,1,0:T(8,128)(2,1)S(1)}, u32[]{:S(2)}, u32[]{:S(2)}) collective-permute-start(bf16[2,2,64,256]{3,2,1,0:T(8,128)(2,1)S(1)} %pad_maximum_fusion.2), channel_id=1, source_target_pairs={{0,2},{1,3},{2,0},{3,1},{4,6},{5,7},{6,4},{7,5},{8,10},{9,11},{10,... | collective-permute-start | bytes 393224 | tf_op jit(solution)/shard_map/ppermute | solution.py:23
  3.4 10.1 %collective-permute-start.5 = (bf16[2,2,64,256]{3,2,1,0:T(8,128)(2,1)S(1)}, bf16[2,2,64,256]{3,2,1,0:T(8,128)(2,1)S(1)}, u32[]{:S(2)}, u32[]{:S(2)}) collective-permute-start(bf16[2,2,64,256]{3,2,1,0:T(8,128)(2,1)S(1)} %pad_maximum_fusion.1.refs_0_), channel_id=1, source_target_pairs={{0,4},{1,5},{2,6},{3,7},{4,8},{5,9},{6,10},{7,11},{8,12},{9,13},{1... | collective-permute-start | bytes 393224 | tf_op jit(solution)/shard_map/ppermute | solution.py:23
  5.0 8.6 %collective-permute-start.6 = (bf16[2,2,64,256]{3,2,1,0:T(8,128)(2,1)S(1)}, bf16[2,2,64,256]{3,2,1,0:T(8,128)(2,1)S(1)}, u32[]{:S(2)}, u32[]{:S(2)}) collective-permute-start(bf16[2,2,64,256]{3,2,1,0:T(8,128)(2,1)S(1)} %pad_maximum_fusion.2), channel_id=1, source_target_pairs={{0,6},{1,7},{2,4},{3,5},{4,10},{5,11},{6,8},{7,9},{8,14},{9,15},{1... | collective-permute-start | bytes 393224 | tf_op jit(solution)/shard_map/ppermute | solution.py:23
  7.5 9.5 %collective-permute-start.7 = (bf16[2,2,64,256]{3,2,1,0:T(8,128)(2,1)S(1)}, bf16[2,2,64,256]{3,2,1,0:T(8,128)(2,1)S(1)}, u32[]{:S(2)}, u32[]{:S(2)}) collective-permute-start(bf16[2,2,64,256]{3,2,1,0:T(8,128)(2,1)S(1)} %pad_maximum_fusion.1.refs_0_), channel_id=1, source_target_pairs={{0,8},{1,9},{2,10},{3,11},{4,12},{5,13},{6,14},{7,15},{8,16},{9,17... | collective-permute-start | bytes 393224 | tf_op jit(solution)/shard_map/ppermute | solution.py:23
  9.0 11.3 %collective-permute-start.8 = (bf16[2,2,64,256]{3,2,1,0:T(8,128)(2,1)S(1)}, bf16[2,2,64,256]{3,2,1,0:T(8,128)(2,1)S(1)}, u32[]{:S(2)}, u32[]{:S(2)}) collective-permute-start(bf16[2,2,64,256]{3,2,1,0:T(8,128)(2,1)S(1)} %pad_maximum_fusion.2), channel_id=1, source_target_pairs={{0,10},{1,11},{2,8},{3,9},{4,14},{5,15},{6,12},{7,13},{8,18},{9,19... | collective-permute-start | bytes 393224 | tf_op jit(solution)/shard_map/ppermute | solution.py:23
